TPU v7x, 32 devices: a whole 2x2x4 slice. The times are simulated.
32 devices in a mesh: gx: 4 (over x, core), gy: 8 (over z, y).
Axes of the slice: x: 2, y: 2, z: 4, core: 2. Of those that a mesh axis runs over, the one named last changes fastest.
Arguments:
- fields: float32 [8192, 2, 1024], P(('gx', 'gy')), may hold values from -6 to 6
- aperture: float32 [8192, 1024], P(('gx', 'gy')), may hold values from 0.1 to 1
- source: float32 [8192, 2, 1024], P(('gx', 'gy')), may hold values from -6 to 6
- storage: float32 [8192, 2], P(('gx', 'gy')), may hold values from 0.02 to 0.5
- coarse_weight: float32 [25088], replicated, may hold values from 0.3 to 3
- source_slot: int32 [131072], P(('gx', 'gy')), may hold values from 0 to 255
- source_edge: int32 [131072], P(('gx', 'gy')), may hold values from 0 to 3
- destination: int32 [131072, 1], P(('gx', 'gy')), may hold values from 0 to 31; in each aligned block of 4096 rows (0 to 4095, 4096 to 8191, ...) at most 128 rows name the same one
- target_frac: int32 [131072], P(('gx', 'gy')), may hold values from 0 to 255
- target_edge: int32 [131072], P(('gx', 'gy')), may hold values from 0 to 3
- coarse_index: int32 [131072], P(('gx', 'gy')), may hold values from 0 to 25087, as said below
Outputs:
- fields_out: float32 [8192, 2, 1024], P(('gx', 'gy'))
- coarse_out: float32 [25088], replicated
Inputs may be any that keep to these rules, and one draw needn't show every extreme that they name: In the records of one device no destination occurs more than 128 times, and some destination occurs exactly 128 times. `coarse_index`: A record of device d names a coarse unknown of d * 784 to (d + 1) * 784 - 1.
All inputs are finite; a program needn't handle non-finite values.
Results may differ from a plain program's by a relative error of at most 0.0001.
Values sent between devices are 32-bit elements; how exact they have to be, the bound alone decides.
A program may use at most 128 MiB of HBM per device.

v0:
```python
import jax
import jax.numpy as jnp
from jax import lax
from jax.sharding import PartitionSpec as P

GRID = 32
ITERS = 2
SWEEPS = 8
SLOT = 128


def edge_rows(fields):
    cells = GRID * GRID
    top = fields[:, :, :GRID]
    bottom = fields[:, :, cells - GRID :]
    left = fields[:, :, 0::GRID]
    right = fields[:, :, GRID - 1 :: GRID]
    return jnp.stack([top, bottom, left, right], 1)


def face_terms(aperture, storage):
    column = jnp.arange(GRID * GRID) % GRID
    a_up = jnp.concatenate([aperture[:, :GRID], aperture[:, :-GRID]], 1)
    a_down = jnp.concatenate([aperture[:, GRID:], aperture[:, -GRID:]], 1)
    a_left = jnp.where(
        column == 0, aperture, jnp.concatenate([aperture[:, :1], aperture[:, :-1]], 1)
    )
    a_right = jnp.where(
        column == GRID - 1, aperture, jnp.concatenate([aperture[:, 1:], aperture[:, -1:]], 1)
    )
    w_up = (0.5 * (aperture + a_up))[:, None, :]
    w_down = (0.5 * (aperture + a_down))[:, None, :]
    w_left = (0.5 * (aperture + a_left))[:, None, :]
    w_right = (0.5 * (aperture + a_right))[:, None, :]
    diag = storage[:, :, None] + w_up + w_down + w_left + w_right
    return (w_up, w_down, w_left, w_right, diag)


def sweeps(fields, boundary, faces, source):
    w_up, w_down, w_left, w_right, diag = faces
    column = jnp.arange(GRID * GRID) % GRID
    top = boundary[:, 0]
    bottom = boundary[:, 1]
    left = jnp.repeat(boundary[:, 2], GRID, axis=-1)
    right = jnp.repeat(boundary[:, 3], GRID, axis=-1)
    for sweep in range(SWEEPS):
        upper = jnp.concatenate([top, fields[:, :, :-GRID]], -1)
        lower = jnp.concatenate([fields[:, :, GRID:], bottom], -1)
        west = jnp.where(
            column == 0, left, jnp.concatenate([fields[:, :, :1], fields[:, :, :-1]], -1)
        )
        east = jnp.where(
            column == GRID - 1, right, jnp.concatenate([fields[:, :, 1:], fields[:, :, -1:]], -1)
        )
        fields = (source + w_up * upper + w_down * lower + w_left * west + w_right * east) / diag
    return fields


def coarse_collect(mismatch, offsets, width):
    group = 8
    peers = mismatch.shape[0]
    blocks_m = mismatch.reshape(peers // group, group, -1)
    blocks_o = offsets.reshape(peers // group, group, -1)
    columns = jnp.arange(width, dtype=jnp.int32)

    def one_block(pair):
        values, local = pair
        table = (local[:, :, None] == columns[None, None, :]).astype(jnp.float32)
        return jnp.einsum("gs,gsc->gc", values, table, precision=lax.Precision.HIGHEST)

    return lax.map(one_block, (blocks_m, blocks_o)).reshape(peers, width)


def coarse_pick(correction_blocks, offsets, width):
    group = 8
    peers = offsets.shape[0]
    blocks_c = correction_blocks.reshape(peers // group, group, width)
    blocks_o = offsets.reshape(peers // group, group, -1)
    columns = jnp.arange(width, dtype=jnp.int32)

    def one_block(pair):
        values, local = pair
        table = (local[:, :, None] == columns[None, None, :]).astype(jnp.float32)
        return jnp.einsum("gsc,gc->gs", table, values, precision=lax.Precision.HIGHEST)

    return lax.map(one_block, (blocks_c, blocks_o)).reshape(peers, -1)


def shards(
    fields,
    aperture,
    source,
    storage,
    coarse_weight,
    source_slot,
    source_edge,
    destination,
    target_frac,
    target_edge,
    coarse_index,
):
    fracs = fields.shape[0]
    width = 2 * GRID
    peers = lax.axis_size(("gx", "gy"))
    slots = SLOT
    coarse = coarse_weight.shape[0]
    per_dev = coarse // peers
    target_dev = destination[:, 0]
    onehot = (target_dev[:, None] == jnp.arange(peers, dtype=jnp.int32)[None, :]).astype(jnp.int32)
    place = jnp.sum(jnp.cumsum(onehot, 0) * onehot, 1) - 1
    packed = jnp.stack([target_frac * 4 + target_edge, coarse_index], 1)
    labels = jnp.full((peers, 2, slots), -1, jnp.int32).at[target_dev, :, place].set(packed)
    arrived = lax.all_to_all(labels, ("gx", "gy"), split_axis=0, concat_axis=0, tiled=True)
    target_flat = arrived[:, 0, :].reshape(-1)
    valid = target_flat >= 0
    weight = valid.astype(jnp.float32)
    peer_base = (jnp.arange(peers, dtype=jnp.int32) * per_dev)[:, None]
    offsets = jnp.where(arrived[:, 1, :] >= 0, arrived[:, 1, :] - peer_base, -1)
    edge_ids = jnp.arange(fracs * 4, dtype=jnp.int32)
    recv_table = (target_flat[:, None] == edge_ids[None, :]).astype(jnp.float32)
    counts = jnp.sum(recv_table, 0)
    sender = source_slot * 4 + source_edge
    slot_record = (
        jnp.full((peers, slots), -1, jnp.int32).at[target_dev, place].set(sender).reshape(-1)
    )
    send_table = (slot_record[:, None] == edge_ids[None, :]).astype(jnp.float32)
    faces = face_terms(aperture, storage)
    correction = jnp.zeros((coarse,), jnp.float32)
    for step in range(ITERS):
        edges = edge_rows(fields).reshape(fracs * 4, width)
        outgoing = jnp.dot(send_table, edges, precision=lax.Precision.HIGHEST).reshape(
            peers, slots, width
        )
        received = lax.all_to_all(outgoing, ("gx", "gy"), split_axis=0, concat_axis=0, tiled=True)
        incoming_rows = received.reshape(peers * slots, width)
        edge_mean = jnp.mean(edges[:, :GRID], axis=1)
        own_mean = jnp.dot(recv_table, edge_mean, precision=lax.Precision.HIGHEST)
        mismatch = weight * (jnp.mean(incoming_rows[:, :GRID], axis=1) - own_mean)
        partial_sum = coarse_collect(mismatch.reshape(peers, slots), offsets, per_dev).reshape(
            coarse
        )
        correction = coarse_weight * lax.psum(partial_sum, ("gx", "gy"))
        slot_value = coarse_pick(correction.reshape(peers, per_dev), offsets, per_dev).reshape(-1)
        values = (incoming_rows + slot_value[:, None]) * weight[:, None]
        incoming = lax.dot_general(
            recv_table, values, (((0,), (0,)), ((), ())), precision=lax.Precision.HIGHEST
        )
        boundary = ((edges + incoming) / (1.0 + counts)[:, None]).reshape(fracs, 4, 2, GRID)
        fields = sweeps(fields, boundary, faces, source)
    return (fields, correction)


def solution(mesh):
    return jax.shard_map(
        shards,
        mesh=mesh,
        in_specs=(
            P(("gx", "gy"), None, None),
            P(("gx", "gy"), None),
            P(("gx", "gy"), None, None),
            P(("gx", "gy"), None),
            P(),
            P(("gx", "gy")),
            P(("gx", "gy")),
            P(("gx", "gy"), None),
            P(("gx", "gy")),
            P(("gx", "gy")),
            P(("gx", "gy")),
        ),
        out_specs=(P(("gx", "gy"), None, None), P()),
        check_vma=False,
    )
```

profile of v0, /device:TPU:0, one launch (start us, length us, event | category | flops | bytes accessed | tf_op | source)
XLA Modules:
  0.0 610.8 jit_solution(3398972177324376998)
XLA Ops:
  8.0 9.2 %reduce-window.6 = s32[32,32,128]{2,1,0:T(8,128)S(1)} reduce-window(s32[32,32,128]{2,1,0:T(8,128)S(1)} %fusion.199, s32[]{:T(128)} %copy.361), window={size=1x1x128 pad=0_0x0_0x127_0}, to_apply=%region_0.0 | reduce-window | flops 16646144 | bytes 1048580 | tf_op jit(solution)/shard_map/reduce-window
  21.2 12.4 %scatter_custom_fusion = s32[4096,2]{1,0:T(8,128)} fusion(s32[4096]{0:T(1024)S(1)} %broadcast_select_fusion, s32[4096,2]{1,0:T(8,128)} %copy.217, s32[]{:T(128)} %constant.90.clone.1), kind=kCustom, calls=%fused_computation.271 | custom fusion | bytes 33280
  36.6 7.4 %all-to-all-start = ((s32[32,2,128]{2,1,0:T(2,128)}), s32[32,2,128]{2,1,0:T(2,128)}, u32[]{:S(2)}, u32[]{:S(2)}) async-start(s32[32,2,128]{2,1,0:T(2,128)} %bitcast.12), calls=%async_computation | async-start | bytes 65536 | tf_op jit(solution)/shard_map/all_to_all | solution.py:113
  45.1 8.6 %slice.389 = f32[256,2,32]{2,1,0:T(2,128)} slice(f32[256,2,1024]{2,1,0:T(2,128)S(1)} %copy-done.8), slice={[0:256:1], [0:2:1], [0:1024:32]} | slice | bytes 131072 | tf_op jit(solution)/shard_map/slice | solution.py:16
  53.7 8.1 %slice.390 = f32[256,2,32]{2,1,0:T(2,128)S(1)} slice(f32[256,2,1024]{2,1,0:T(2,128)S(1)} %copy-done.8), slice={[0:256:1], [0:2:1], [31:1024:32]} | slice | bytes 131072 | tf_op jit(solution)/shard_map/slice | solution.py:17
  66.8 4.9 fusion.253
  76.4 15.9 %scatter_custom_fusion.1 = s32[4096]{0:T(1024)S(1)} fusion(s32[4096]{0:T(1024)} %copy-done.35, s32[4096]{0:T(1024)S(1)} %multiply_add_fusion, s32[]{:T(128)} %constant.90.clone.1), kind=kCustom, calls=%fused_computation.317 | custom fusion | bytes 16896
  92.4 4.9 fusion.183
  97.3 9.6 %fusion.25 = f32[32,128,64]{1,2,0:T(8,128)} fusion(s32[32,128]{1,0:T(8,128)S(1)} %bitcast.406, f32[1024,64]{1,0:T(8,128)S(1)} %reshape.149), kind=kOutput, calls=%fused_computation.41 | convolution fusion | flops 3225419776 | bytes 1327104 | tf_op jit(solution)/shard_map/dot_general | solution.py:131
  117.4 4.1 copy.299
  121.5 4.1 copy.300
  125.7 5.9 all-to-all-start.1
  132.1 7.1 %fusion.255 = (f32[256,2,992]{2,1,0:T(2,128)}, f32[256,2,992]{2,1,0:T(2,128)}) fusion(f32[256,2,1024]{2,1,0:T(2,128)} %param.19), kind=kLoop, calls=%fused_computation.378 | loop fusion | bytes 8126464 | tf_op jit(solution)/shard_map/slice | solution.py:48
  139.2 4.1 copy.296
  143.3 4.1 copy.297
  154.1 8.0 %fusion.21 = f32[1,4096]{1,0:T(1,128)S(1)} fusion(f32[1024,1]{0,1:T(1,128)S(1)} %bitcast.412, s32[4096]{0:T(1024)S(1)} %bitcast.397), kind=kOutput, calls=%fused_computation.38 | convolution fusion | flops 54525952 | bytes 36864 | tf_op jit(solution)/shard_map/dot_general | solution.py:137
  165.5 5.6 while.44
  172.6 121.2 %all-reduce.3.cloned.1.call-done = f32[25088]{0:T(1024)} async-done(((f32[25088]{0:T(1024)}), f32[25088]{0:T(1024)}) %all-reduce.3.cloned.1.call-update) | async-done | bytes 100368 | tf_op jit(solution)/shard_map/psum | solution.py:142
  295.5 10.4 %while.45 = (s32[]{:T(128)}, f32[4,8,128]{2,1,0:T(8,128)}, s32[4,8,128]{2,1,0:T(8,128)S(1)}, f32[4,8,784]{2,1,0:T(8,128)S(1)}, s32[]{:T(128)}) while((s32[]{:T(128)}, f32[4,8,128]{2,1,0:T(8,128)}, s32[4,8,128]{2,1,0:T(8,128)S(1)}, f32[4,8,784]{2,1,0:T(8,128)S(1)}, s32[]{:T(128)}) %tuple.161), condition=%wide.region_11.12_spmd.clone, body=%wide.region_10.11_spmd.clone.sunk | while | flops 10436610 | bytes 100421 | solution.py:86
  305.9 8.4 %fusion.180 = f32[1024,64]{0,1:T(8,128)} fusion(f32[1024,64]{0,1:T(8,128)S(1)} %copy-done.23, s32[4096]{0:T(1024)} %bitcast.400, f32[4096]{0:T(1024)} %convert_element_type.21, f32[4096]{0:T(1024)} %bitcast.410, f32[1024]{0:T(1024)S(1)} %broadcast_add_fusion.3, f32[32,128,64]{1,2,0:T(8,128)} %all-to-all-done.1), kind=kOutput, calls=%fused_computation.262 | convolution fusion | flops 3226075136 | bytes 1626112 | tf_op jit(solution)/shard_map/dot_general | solution.py:145
  324.3 5.5 fusion.136
  368.5 10.7 %fusion.23 = f32[32,128,64]{1,2,0:T(8,128)} fusion(s32[32,128]{1,0:T(8,128)} %bitcast.407, f32[1024,64]{1,0:T(8,128)} %reshape.155), kind=kOutput, calls=%fused_computation.40 | convolution fusion | flops 3225419776 | bytes 1327104 | tf_op jit(solution)/shard_map/dot_general | solution.py:131
  379.2 5.6 all-to-all-start.2
  386.2 8.2 %fusion.19 = f32[1,4096]{1,0:T(1,128)S(1)} fusion(f32[1024,1]{0,1:T(1,128)S(1)} %bitcast.413, s32[4096]{0:T(1024)S(1)} %bitcast.401), kind=kOutput, calls=%fused_computation.36 | convolution fusion | flops 54525952 | bytes 36864 | tf_op jit(solution)/shard_map/dot_general | solution.py:137
  399.0 13.4 %all-to-all-done.2 = f32[32,128,64]{1,2,0:T(8,128)} async-done(((f32[32,128,64]{1,2,0:T(8,128)}), f32[32,128,64]{1,2,0:T(8,128)}, u32[]{:S(2)}, u32[]{:S(2)}) %all-to-all-start.2) | async-done | bytes 1048608 | tf_op jit(solution)/shard_map/all_to_all | solution.py:134
  413.8 5.6 while.46
  423.5 115.1 %all-reduce.5.cloned.1.call-done = f32[25088]{0:T(1024)} async-done(((f32[25088]{0:T(1024)}), f32[25088]{0:T(1024)}) %all-reduce.5.cloned.1.call-update) | async-done | bytes 100368 | tf_op jit(solution)/shard_map/psum | solution.py:142
  540.1 7.9 %while.47 = (s32[]{:T(128)}, f32[4,8,128]{2,1,0:T(8,128)S(1)}, s32[4,8,128]{2,1,0:T(8,128)S(1)}, f32[4,8,784]{2,1,0:T(8,128)S(1)}, s32[]{:T(128)}) while((s32[]{:T(128)}, f32[4,8,128]{2,1,0:T(8,128)S(1)}, s32[4,8,128]{2,1,0:T(8,128)S(1)}, f32[4,8,784]{2,1,0:T(8,128)S(1)}, s32[]{:T(128)}) %tuple.163), condition=%wide.region_19.20_spmd.clone, body=%wide.region_18.19_spmd.clone.sunk | while | flops 10436610 | bytes 99913 | solution.py:86
  548.1 7.6 %fusion.179 = f32[1024,64]{0,1:T(8,128)S(1)} fusion(f32[1024,64]{0,1:T(8,128)} %copy.263, s32[4096]{0:T(1024)S(1)} %bitcast.402, f32[4096]{0:T(1024)S(1)} %bitcast.409, f32[4096]{0:T(1024)S(1)} %copy-done.33, f32[1024]{0:T(1024)S(1)} %copy-done.39, f32[32,128,64]{1,2,0:T(8,128)} %all-to-all-done.2), kind=kOutput, calls=%fused_computation.261 | convolution fusion | flops 3226075136 | bytes 1626112 | tf_op jit(solution)/shard_map/dot_general | solution.py:145
  564.8 5.8 fusion.80
  595.7 3.9 fusion.38
  599.6 4.1 copy.277
  (296 shorter events, 166.6 us)
Async XLA Ops:
  7.2 11.7 %copy-start.41 = (s32[2]{0:T(128)S(1)}, s32[2]{0:T(128)}, u32[]{:S(2)}) copy-start(s32[2]{0:T(128)} %constant.101) | copy-start | bytes 28
  7.2 11.8 %copy-start.40 = (s32[2]{0:T(128)S(1)}, s32[2]{0:T(128)}, u32[]{:S(2)}) copy-start(s32[2]{0:T(128)} %constant.104) | copy-start | bytes 28
  7.2 11.3 %copy-start.24 = (s32[4096,1]{0,1:T(1,128)S(1)}, s32[4096,1]{0,1:T(1,128)}, u32[]{:S(2)}) copy-start(s32[4096,1]{0,1:T(1,128)} %param.26) | copy-start | bytes 49156
  7.2 11.9 %copy-start.30 = (s32[4096]{0:T(1024)S(1)}, s32[4096]{0:T(1024)}, u32[]{:S(2)}) copy-start(s32[4096]{0:T(1024)} %param.27) | copy-start | bytes 49156
  7.2 11.9 %copy-start.29 = (s32[4096]{0:T(1024)S(1)}, s32[4096]{0:T(1024)}, u32[]{:S(2)}) copy-start(s32[4096]{0:T(1024)} %param.28) | copy-start | bytes 49156
  7.2 12.0 %copy-start.36 = (s32[4096]{0:T(1024)S(1)}, s32[4096]{0:T(1024)}, u32[]{:S(2)}) copy-start(s32[4096]{0:T(1024)} %param.29) | copy-start | bytes 49156
  21.2 12.4 %copy-start.35 = (s32[4096]{0:T(1024)}, s32[4096]{0:T(1024)S(1)}, u32[]{:S(2)}) copy-start(s32[4096]{0:T(1024)S(1)} %broadcast_select_fusion) | copy-start | bytes 49156
  21.2 22.8 %copy-start.8 = (f32[256,2,1024]{2,1,0:T(2,128)S(1)}, f32[256,2,1024]{2,1,0:T(2,128)}, u32[]{:S(2)}) copy-start(f32[256,2,1024]{2,1,0:T(2,128)} %param.19) | copy-start | bytes 6291460
  33.6 28.2 %copy-start.9 = (f32[256,1024]{1,0:T(8,128)S(1)}, f32[256,1024]{1,0:T(8,128)}, u32[]{:S(2)}) copy-start(f32[256,1024]{1,0:T(8,128)} %param.20) | copy-start | bytes 3145732
  36.6 89.1 %all-to-all-start = ((s32[32,2,128]{2,1,0:T(2,128)}), s32[32,2,128]{2,1,0:T(2,128)}, u32[]{:S(2)}, u32[]{:S(2)}) async-start(s32[32,2,128]{2,1,0:T(2,128)} %bitcast.12), calls=%async_computation | async-start | bytes 65536 | tf_op jit(solution)/shard_map/all_to_all | solution.py:113
  61.8 30.5 %copy-start.17 = (pred[1024]{0:T(1024)(128)(4,1)}, pred[1024]{0:T(1024)(128)(4,1)S(1)}, u32[]{:S(2)}) copy-start(pred[1024]{0:T(1024)(128)(4,1)S(1)} %get-tuple-element.322) | copy-start | bytes 3076
  61.8 30.5 %copy-start.20 = (pred[1024]{0:T(1024)(128)(4,1)}, pred[1024]{0:T(1024)(128)(4,1)S(1)}, u32[]{:S(2)}) copy-start(pred[1024]{0:T(1024)(128)(4,1)S(1)} %get-tuple-element.323) | copy-start | bytes 3076
  76.4 30.5 %copy-start.10 = (f32[1024,64]{1,0:T(8,128)}, f32[1024,64]{1,0:T(8,128)S(1)}, u32[]{:S(2)}) copy-start(f32[1024,64]{1,0:T(8,128)S(1)} %reshape.149) | copy-start | bytes 786436
  125.7 38.4 %all-to-all-start.1 = ((f32[32,128,64]{1,2,0:T(8,128)}), f32[32,128,64]{1,2,0:T(8,128)}, u32[]{:S(2)}, u32[]{:S(2)}) async-start(f32[32,128,64]{1,2,0:T(8,128)} %fusion.25), calls=%async_computation.1 | async-start | bytes 2097152 | tf_op jit(solution)/shard_map/all_to_all | solution.py:134
  131.5 162.3 %all-reduce.3.cloned.1.call-start = ((), (), s32[]{:S(2)}) async-start(), calls=%async_computation.3 | async-start | bytes 204800 | tf_op jit(solution)/shard_map/psum | solution.py:142
  154.0 11.4 %copy-start.25 = (s32[32,1,128]{2,1,0:T(1,128)}, s32[32,1,128]{2,1,0:T(1,128)S(1)}, u32[]{:S(2)}) copy-start(s32[32,1,128]{2,1,0:T(1,128)S(1)} %get-tuple-element.317) | copy-start | bytes 49156
  165.4 6.5 %copy-start.27 = (pred[4096]{0:T(1024)(128)(4,1)}, pred[4096]{0:T(1024)(128)(4,1)S(1)}, u32[]{:S(2)}) copy-start(pred[4096]{0:T(1024)(128)(4,1)S(1)} %get-tuple-element.195) | copy-start | bytes 12292
  165.5 128.3 %copy-start.14 = (f32[25088]{0:T(1024)S(1)}, f32[25088]{0:T(1024)}, u32[]{:S(2)}) copy-start(f32[25088]{0:T(1024)} %param.23) | copy-start | bytes 301060
  171.9 134.0 %copy-start.38 = (f32[1024]{0:T(1024)}, f32[1024]{0:T(1024)S(1)}, u32[]{:S(2)}) copy-start(f32[1024]{0:T(1024)S(1)} %broadcast_add_fusion.3) | copy-start | bytes 12292
  295.5 10.5 %copy-start.23 = (f32[1024,64]{0,1:T(8,128)S(1)}, f32[1024,64]{0,1:T(8,128)}, u32[]{:S(2)}) copy-start(f32[1024,64]{0,1:T(8,128)} %copy.223) | copy-start | bytes 786436
  379.2 6.9 %copy-start.26 = (s32[32,1,128]{2,1,0:T(1,128)S(1)}, s32[32,1,128]{2,1,0:T(1,128)}, u32[]{:S(2)}) copy-start(s32[32,1,128]{2,1,0:T(1,128)} %copy-done.25) | copy-start | bytes 49156
  379.2 33.2 %all-to-all-start.2 = ((f32[32,128,64]{1,2,0:T(8,128)}), f32[32,128,64]{1,2,0:T(8,128)}, u32[]{:S(2)}, u32[]{:S(2)}) async-start(f32[32,128,64]{1,2,0:T(8,128)} %fusion.23), calls=%async_computation.2 | async-start | bytes 2097152 | tf_op jit(solution)/shard_map/all_to_all | solution.py:134
  384.8 153.8 %all-reduce.5.cloned.1.call-start = ((), (), s32[]{:S(2)}) async-start(), calls=%async_computation.4 | async-start | bytes 204800 | tf_op jit(solution)/shard_map/psum | solution.py:142
  386.1 8.2 %copy-start.7 = (f32[256,2,1024]{0,2,1:T(8,128)S(1)}, f32[256,2,1024]{0,2,1:T(8,128)}, u32[]{:S(2)}) copy-start(f32[256,2,1024]{0,2,1:T(8,128)} %copy-done.6) | copy-start | bytes 6291460
  399.0 14.7 %copy-start.28 = (pred[4096]{0:T(1024)(128)(4,1)S(1)}, pred[4096]{0:T(1024)(128)(4,1)}, u32[]{:S(2)}) copy-start(pred[4096]{0:T(1024)(128)(4,1)} %copy-done.27) | copy-start | bytes 12292
  413.8 124.8 %copy-start.15 = (f32[25088]{0:T(1024)S(1)}, f32[25088]{0:T(1024)}, u32[]{:S(2)}) copy-start(f32[25088]{0:T(1024)} %param.23) | copy-start | bytes 301060
  539.6 8.4 %copy-start.33 = (f32[4096]{0:T(1024)S(1)}, f32[4096]{0:T(1024)}, u32[]{:S(2)}) copy-start(f32[4096]{0:T(1024)} %convert_element_type.21) | copy-start | bytes 49156
  539.7 8.4 %copy-start.39 = (f32[1024]{0:T(1024)S(1)}, f32[1024]{0:T(1024)}, u32[]{:S(2)}) copy-start(f32[1024]{0:T(1024)} %copy-done.38) | copy-start | bytes 12292
  559.4 5.4 copy-start.13
  559.4 5.5 copy-start.19
  559.4 5.5 copy-start.22
  559.4 5.5 copy-start.37
  (15 other events, 30.9 us)
Sparse Core Ops, SparseCore 0:
  172.0 121.7 all-reduce.2
  420.3 118.1 all-reduce.4
where the time goes:
time: 621 us; the launch traced here: 611 us
  waiting for transfers between devices  250 us (40%)
  local copies, waits for them, and re-layouts  167 us (27%)
  other arithmetic  79.7 us (13%)
  matrix products  79.1 us (13%)
  starting transfers between devices  19.5 us (3%)
  between operations  15.5 us (2%)
    psum x2, waiting for transfers between devices, shards(): correction = coarse_weight * lax.psum(partial_sum, ('gx', 'gy'))  236 us
    unnamed x101, local copies, waits for them, and re-layouts  66.4 us
    div x16, other arithmetic, sweeps(): (source + w_up * upper + w_down * lower + w_left * west + w_right * east)...  55.8 us
    dot_general x2, matrix products, shards(): jnp.dot(send_table, edges, precision=lax.Precision.HIGHEST)  20.3 us
    dot_general x2, matrix products, shards(): own_mean = jnp.dot(recv_table, edge_mean, precision=lax.Precision.HIGHEST)  16.3 us
    dot_general x2, matrix products, shards(): lax.dot_general(recv_table, values, (((0,), (0,)), ((), ())), precision=l...  16 us
    dot_general x8, matrix products, one_block(): jnp.einsum('gsc,gc->gs', table, values, precision=lax.Precision.HIGHEST)  15.6 us
    slice x16, local copies, waits for them, and re-layouts, sweeps(): lower = jnp.concatenate([fields[:, :, GRID:], bottom], -1)  14.3 us
  transfers between devices with their start and end apart: 5, of which 3 were waited for; matrix products, arithmetic and copies ran while one was open for 22% of the time, Pallas kernels for 0%

commit v1 on v0

v1 whole, which is shorter than its diff:
```python
import functools

import jax
import jax.numpy as jnp
from jax import lax
from jax.experimental import pallas as pl
from jax.experimental.pallas import tpu as pltpu
from jax.sharding import PartitionSpec as P

GRID = 32
ITERS = 2
SWEEPS = 8
SLOT = 128
LANES = 128
TILES = GRID * GRID // LANES
AXES = ("gx", "gy")
NT = (((1,), (1,)), ((), ()))
NN = (((1,), (0,)), ((), ()))


def dot(a, b, dims):
    return lax.dot_general(a, b, dims, preferred_element_type=jnp.float32)


def dot_exact(a, b, dims):
    return lax.dot_general(
        a, b, dims, precision=lax.Precision.HIGHEST, preferred_element_type=jnp.float32
    )


def split3(x):
    high = x.astype(jnp.bfloat16)
    rest = x - high.astype(jnp.float32)
    mid = rest.astype(jnp.bfloat16)
    low = (rest - mid.astype(jnp.float32)).astype(jnp.bfloat16)
    return high, mid, low


def iota(shape, dim):
    return lax.broadcasted_iota(jnp.int32, shape, dim)


def equal(a, b, dtype=jnp.bfloat16):
    return jnp.where(a == b, 1.0, 0.0).astype(dtype)


def slots_body(peers, fracs, record_ref, sender_ref, target_ref, coarse_ref):
    chunk = 512
    count = record_ref.shape[1]
    upto = (iota((chunk, chunk), 0) <= iota((chunk, chunk), 1)).astype(jnp.float32)
    upto = upto.astype(jnp.bfloat16)
    base = jnp.zeros((peers, 1), jnp.float32)
    total = jnp.zeros((6 * peers, SLOT), jnp.float32)
    for start in range(0, count, chunk):
        rows = [record_ref[i : i + 1, start : start + chunk] for i in range(7)]
        onehot = equal(iota((peers, chunk), 0), rows[0], jnp.float32)
        running = dot(onehot.astype(jnp.bfloat16), upto, NN)
        place = jnp.sum(onehot * (running + base), 0, keepdims=True) - 1.0
        base = base + running[:, chunk - 1 :]
        at_place = equal(iota((SLOT, chunk), 0), place.astype(jnp.int32))
        parts = [onehot * rows[i].astype(jnp.float32) for i in range(1, 7)]
        total = total + dot(jnp.concatenate(parts, 0).astype(jnp.bfloat16), at_place, NT)
    table = (total + 0.5).astype(jnp.int32)
    pieces = [table[i * peers : (i + 1) * peers] for i in range(6)]
    valid = pieces[3] > 0
    sender_ref[...] = jnp.where(valid, pieces[1] * fracs + pieces[0], -1)
    target_ref[...] = jnp.where(valid, (pieces[3] - 1) * fracs + pieces[2], -1)
    coarse_ref[...] = jnp.where(valid, pieces[4] * LANES + pieces[5], -1)


def edge_selector(tile):
    row = iota((4 * GRID, LANES), 0)
    k, edge = row & (GRID - 1), row >> 5
    cell = jnp.where(
        edge == 0,
        k,
        jnp.where(edge == 1, GRID * (GRID - 1) + k, k * GRID + (edge - 2) * (GRID - 1)),
    )
    return (iota((4 * GRID, LANES), 1) + tile * LANES) == cell


def edge_and_frac(code, fracs):
    shift = fracs.bit_length() - 1
    return jnp.where(code >= 0, code >> shift, -1), jnp.where(code >= 0, code & (fracs - 1), -1)


def edges_body(peers, fracs, fields_ref, sender_ref, edges_ref, rows_ref, mean_ref, split_ref):
    for c in range(2):
        total = jnp.zeros((4 * GRID, fracs), jnp.float32)
        for tile in range(TILES):
            cells = fields_ref[pl.ds(tile * 2 + c, fracs, stride=2 * TILES), :]
            selector = edge_selector(tile).astype(jnp.float32).astype(jnp.bfloat16)
            for part in split3(cells):
                total = total + dot(selector, part, NT)
        edges_ref[c * 4 * GRID : (c + 1) * 4 * GRID, :] = total
        for i, part in enumerate(split3(total)):
            start = i * 8 * GRID + c * 4 * GRID
            split_ref[start : start + 4 * GRID, :] = part

    def one_peer(d, carry):
        edge, frac = edge_and_frac(sender_ref[pl.ds(d, 1), :], fracs)
        onehot = equal(iota((fracs, SLOT), 0), frac)
        picked = dot(split_ref[...], onehot, NN)
        picked = picked[: 8 * GRID] + picked[8 * GRID : 16 * GRID] + picked[16 * GRID :]
        for c in range(2):
            row = jnp.zeros((GRID, SLOT), jnp.float32)
            for e in range(4):
                start = c * 4 * GRID + e * GRID
                row = jnp.where(edge == e, picked[start : start + GRID], row)
            rows_ref[d, c * GRID : (c + 1) * GRID, :] = row
            if c == 0:
                mean_ref[pl.ds(d, 1), :] = jnp.sum(row, 0, keepdims=True) * (1.0 / GRID)
        return carry

    lax.fori_loop(0, peers, one_peer, 0)


def means_body(peers, fracs, edges_ref, arrived_ref, mean_ref):
    means = [
        jnp.sum(edges_ref[e * GRID : (e + 1) * GRID, :], 0, keepdims=True) * (1.0 / GRID)
        for e in range(4)
    ]
    table = jnp.concatenate(means + means, 0)
    parts = jnp.concatenate(
        [p.astype(jnp.float32) for p in split3(table)] + [jnp.zeros_like(table)], 0
    ).astype(jnp.bfloat16)

    def one_peer(d, carry):
        edge, frac = edge_and_frac(arrived_ref[pl.ds(d, 1), :], fracs)
        picked = dot(parts, equal(iota((fracs, SLOT), 0), frac), NN)
        picked = picked[:8] + picked[8:16] + picked[16:24]
        mine = jnp.where(iota((8, SLOT), 0) == edge, picked, 0.0)
        mean_ref[pl.ds(d, 1), :] = jnp.sum(mine, 0, keepdims=True)
        return carry

    lax.fori_loop(0, peers, one_peer, 0)


def coarse_body(peers, high, mean_ref, other_ref, index_ref, weight_ref, corr_ref, out_ref):
    def tables(d):
        index = index_ref[pl.ds(d, 1), :]
        row = jnp.where(index >= 0, index >> 7, -1)
        lane = jnp.where(index >= 0, index & (LANES - 1), -1)
        return iota((high, SLOT), 0) == row, equal(iota((LANES, SLOT), 0), lane, jnp.float32)

    def collect(d, total):
        rows, lanes = tables(d)
        mismatch = mean_ref[pl.ds(d, 1), :] - other_ref[pl.ds(d, 1), :]
        return total + dot_exact(jnp.where(rows, mismatch, 0.0), lanes, NT)

    residual = lax.fori_loop(0, peers, collect, jnp.zeros((high, LANES), jnp.float32))
    correction = residual * weight_ref[...]
    corr_ref[...] = correction

    def pick(d, carry):
        rows, lanes = tables(d)
        picked = dot_exact(correction, lanes, NN)
        out_ref[pl.ds(d, 1), :] = jnp.sum(jnp.where(rows, picked, 0.0), 0, keepdims=True)
        return carry

    lax.fori_loop(0, peers, pick, 0)


def sweep_body(
    peers,
    fracs,
    rows_ref,
    extra_ref,
    arrived_ref,
    edges_ref,
    fields_ref,
    aperture_ref,
    source_ref,
    storage_ref,
    out_ref,
    sum_ref,
    count_ref,
    border_ref,
    side_ref,
):
    sum_ref[...] = jnp.zeros_like(sum_ref)
    count_ref[...] = jnp.zeros_like(count_ref)

    def one_peer(d, carry):
        edge, frac = edge_and_frac(arrived_ref[pl.ds(d, 1), :], fracs)
        onehot = equal(iota((fracs, SLOT), 0), frac)
        values = rows_ref[d] + extra_ref[pl.ds(d, 1), :]
        masked = []
        for c in range(2):
            for e in range(4):
                masked.append(jnp.where(edge == e, values[c * GRID : (c + 1) * GRID], 0.0))
        masked = jnp.concatenate(masked, 0)
        total = sum_ref[...]
        for part in split3(masked):
            total = total + dot(part, onehot, NT)
        sum_ref[...] = total
        count_ref[...] += dot(equal(iota((16, SLOT), 0), edge), onehot, NT)
        return carry

    lax.fori_loop(0, peers, one_peer, 0)
    for c in range(2):
        borders = []
        for e in range(4):
            start = (c * 4 + e) * GRID
            total = edges_ref[start : start + GRID, :] + sum_ref[start : start + GRID, :]
            borders.append(total / (1.0 + count_ref[e : e + 1, :]))
        border = jnp.transpose(jnp.concatenate(borders, 0))
        border_ref[c] = border
        parts = split3(border)
        for tile in range(TILES):
            row = iota((4 * GRID, LANES), 0)
            inject = edge_selector(tile) & (row >= 2 * GRID)
            inject = inject.astype(jnp.float32).astype(jnp.bfloat16)
            side = dot(parts[0], inject, NN) + dot(parts[1], inject, NN) + dot(parts[2], inject, NN)
            side_ref[c, :, tile * LANES : (tile + 1) * LANES] = side

    lane = iota((8, LANES), 1)
    column = lane & (GRID - 1)
    first, last = lane < GRID, lane >= LANES - GRID
    west_end, east_end = column == 0, column == GRID - 1

    def neighbours(x):
        down = [pltpu.roll(v, GRID, 1) for v in x]
        up = [pltpu.roll(v, LANES - GRID, 1) for v in x]
        above = [down[0]] + [jnp.where(first, down[t - 1], down[t]) for t in range(1, TILES)]
        below = [jnp.where(last, up[t + 1], up[t]) for t in range(TILES - 1)] + [up[-1]]
        left = [pltpu.roll(v, 1, 1) for v in x]
        right = [pltpu.roll(v, LANES - 1, 1) for v in x]
        return above, below, left, right

    def one_tile(i, carry):
        start = pl.multiple_of(i * 8, 8)
        here = pl.ds(start, 8)
        a = [aperture_ref[here, t * LANES : (t + 1) * LANES] for t in range(TILES)]
        above, below, left, right = neighbours(a)
        above[0] = jnp.where(first, a[0], above[0])
        below[-1] = jnp.where(last, a[-1], below[-1])
        w_up = [0.5 * (a[t] + above[t]) for t in range(TILES)]
        w_down = [0.5 * (a[t] + below[t]) for t in range(TILES)]
        w_left = [0.5 * (a[t] + jnp.where(west_end, a[t], left[t])) for t in range(TILES)]
        w_right = [0.5 * (a[t] + jnp.where(east_end, a[t], right[t])) for t in range(TILES)]
        for c in range(2):
            store = storage_ref[here, c : c + 1]
            border = border_ref[c, here, :]
            x, s, cu, cd, cl, cr = [], [], [], [], [], []
            for t in range(TILES):
                at = pl.ds(start * 2 * TILES + t * 2 + c, 8, stride=2 * TILES)
                inverse = 1.0 / (store + w_up[t] + w_down[t] + w_left[t] + w_right[t])
                side = side_ref[c, here, t * LANES : (t + 1) * LANES]
                value = source_ref[at, :] + side * jnp.where(west_end, w_left[t], w_right[t])
                up, down = w_up[t] * inverse, w_down[t] * inverse
                if t == 0:
                    value = value + jnp.where(first, border * w_up[t], 0.0)
                    up = jnp.where(first, 0.0, up)
                if t == TILES - 1:
                    bottom = pltpu.roll(border, 2 * GRID, 1)
                    value = value + jnp.where(last, bottom * w_down[t], 0.0)
                    down = jnp.where(last, 0.0, down)
                x.append(fields_ref[at, :])
                s.append(value * inverse)
                cu.append(up)
                cd.append(down)
                cl.append(jnp.where(west_end, 0.0, w_left[t] * inverse))
                cr.append(jnp.where(east_end, 0.0, w_right[t] * inverse))
            for sweep in range(SWEEPS):
                above, below, left, right = neighbours(x)
                x = [
                    (s[t] + cu[t] * above[t])
                    + (cd[t] * below[t] + (cl[t] * left[t] + cr[t] * right[t]))
                    for t in range(TILES)
                ]
            for t in range(TILES):
                at = pl.ds(start * 2 * TILES + t * 2 + c, 8, stride=2 * TILES)
                out_ref[at, :] = x[t]
        return carry

    lax.fori_loop(0, fracs // 8, one_tile, 0)


def call(body, shapes, scratch=()):
    return pl.pallas_call(
        body,
        out_shape=[jax.ShapeDtypeStruct(shape, dtype) for shape, dtype in shapes],
        scratch_shapes=list(scratch),
        compiler_params=pltpu.CompilerParams(vmem_limit_bytes=48 * 1024 * 1024),
    )


def exchange(x):
    return lax.all_to_all(x, AXES, split_axis=0, concat_axis=0, tiled=True)


def by_tiles(x):
    fracs = x.shape[0]
    return x.reshape(fracs, 2, TILES, LANES).transpose(0, 2, 1, 3).reshape(-1, LANES)


def shards(
    fields,
    aperture,
    source,
    storage,
    coarse_weight,
    source_slot,
    source_edge,
    destination,
    target_frac,
    target_edge,
    coarse_index,
):
    f32, i32 = jnp.float32, jnp.int32
    fracs = fields.shape[0]
    peers = lax.axis_size(AXES)
    coarse = coarse_weight.shape[0]
    per_dev = coarse // peers
    high = -(-per_dev // (8 * LANES)) * 8
    first = lax.axis_index(AXES) * per_dev
    local = coarse_index - first
    none = jnp.zeros_like(local)
    records = jnp.stack(
        [
            destination[:, 0],
            source_slot,
            source_edge,
            target_frac,
            target_edge + 1,
            local >> 7,
            local & (LANES - 1),
            none,
        ],
        0,
    )
    weight = lax.dynamic_slice(coarse_weight, (first,), (per_dev,))
    weight = jnp.pad(weight, (0, high * LANES - per_dev)).reshape(high, LANES)
    table = (peers, SLOT)
    sender, target, index = call(
        functools.partial(slots_body, peers, fracs), [(table, i32)] * 3
    )(records)
    arrived = exchange(target)
    state, sources = by_tiles(fields), by_tiles(source)
    for step in range(ITERS):
        edges, rows, mean = call(
            functools.partial(edges_body, peers, fracs),
            [((8 * GRID, fracs), f32), ((peers, 2 * GRID, SLOT), f32), (table, f32)],
            [pltpu.VMEM((24 * GRID, fracs), jnp.bfloat16)],
        )(state, sender)
        rows = exchange(rows)
        (own,) = call(functools.partial(means_body, peers, fracs), [(table, f32)])(edges, arrived)
        correction, extra = call(
            functools.partial(coarse_body, peers, high), [((high, LANES), f32), (table, f32)]
        )(mean, exchange(own), index, weight)
        (state,) = call(
            functools.partial(sweep_body, peers, fracs),
            [(state.shape, f32)],
            [
                pltpu.VMEM((8 * GRID, fracs), f32),
                pltpu.VMEM((16, fracs), f32),
                pltpu.VMEM((2, fracs, 4 * GRID), f32),
                pltpu.VMEM((2, fracs, GRID * GRID), f32),
            ],
        )(rows, exchange(extra), arrived, edges, state, aperture, sources, storage)
    blocks = lax.all_gather(correction, AXES, tiled=True)
    coarse_out = blocks.reshape(peers, high * LANES)[:, :per_dev].reshape(coarse)
    fields_out = state.reshape(fracs, TILES, 2, LANES).transpose(0, 2, 1, 3).reshape(fields.shape)
    return fields_out, coarse_out


def solution(mesh):
    every = P(AXES)
    return jax.shard_map(
        shards,
        mesh=mesh,
        in_specs=(
            P(AXES, None, None),
            P(AXES, None),
            P(AXES, None, None),
            P(AXES, None),
            P(),
            every,
            every,
            P(AXES, None),
            every,
            every,
            every,
        ),
        out_specs=(P(AXES, None, None), P()),
        check_vma=False,
    )
```

time: 621 us -> 346 us (0.56); the launches traced: 611 us -> 345 us
  waiting for transfers between devices: 250 us -> 34.5 us
  Pallas kernels: 0 us -> 161 us
  local copies, waits for them, and re-layouts: 167 us -> 12.9 us
  blocking collectives: 0 us -> 115 us
  matrix products: 79.1 us -> 0 us
  other arithmetic: 79.7 us -> 1.44 us
  between operations: 15.5 us -> 0.77 us
    psum x2 -> x0, waiting for transfers between devices: 236 us -> none  [shards(): correction = coarse_weight * lax.psum(partial_sum, ('gx', 'gy'))]
    pallas_call x0 -> x9, Pallas kernels: none -> 161 us  [the longest x2 101 us: shards(): call(functools.partial(sweep_body, peers, fracs), [(state.shape, f32)], [...]
    all_gather x0 -> x1, blocking collectives: none -> 86.8 us  [shards(): blocks = lax.all_gather(correction, AXES, tiled=True)]
    dot_general x22 -> x0, matrix products: 79.1 us -> none  [the longest x2 20.3 us: shards(): jnp.dot(send_table, edges, precision=lax.Precision.HIGHEST)]
    slice x65 -> x1, local copies, waits for them, and re-layouts: 64.9 us -> 1.54 us  [shards(): blocks.reshape(peers, high * LANES)[:, :per_dev].reshape(coarse)]
    unnamed x101 -> x31, local copies, waits for them, and re-layouts: 66.4 us -> 6.35 us
    div x18 -> x0, other arithmetic: 55.8 us -> none  [the longest x16 55.8 us: sweeps(): (source + w_up * upper + w_down * lower + w_left * west + w_right * east)...]
    all_to_all x0 -> x3, blocking collectives: none -> 27.9 us  [exchange(): return lax.all_to_all(x, AXES, split_axis=0, concat_axis=0, tiled=True)]
  transfers between devices with their start and end apart: 5 -> 4, of which waited for: 3 -> 2; matrix products, arithmetic and copies ran while one was open for 22% -> 2% of each run, Pallas kernels for 0% -> 3%
where the time goes in v1:
time: 346 us; the launch traced here: 345 us
  Pallas kernels  161 us (47%)
  blocking collectives  115 us (33%)
  waiting for transfers between devices  34.5 us (10%)
  starting transfers between devices  19.2 us (6%)
  local copies, waits for them, and re-layouts  12.9 us (4%)
    pallas_call x2, Pallas kernels, shards(): call(functools.partial(sweep_body, peers, fracs), [(state.shape, f32)], [...  101 us
    all_gather x1, blocking collectives, shards(): blocks = lax.all_gather(correction, AXES, tiled=True)  86.8 us
    all_to_all x4, waiting for transfers between devices, exchange(): return lax.all_to_all(x, AXES, split_axis=0, concat_axis=0, tiled=True)  34.5 us
    all_to_all x3, blocking collectives, exchange(): return lax.all_to_all(x, AXES, split_axis=0, concat_axis=0, tiled=True)  27.9 us
    pallas_call x2, Pallas kernels, shards(): call(functools.partial(coarse_body, peers, high), [((high, LANES), f32),...  26 us
    pallas_call x2, Pallas kernels, shards(): call(functools.partial(edges_body, peers, fracs), [((8 * GRID, fracs), f3...  21.2 us
    all_to_all x4, starting transfers between devices, exchange(): return lax.all_to_all(x, AXES, split_axis=0, concat_axis=0, tiled=True)  19.2 us
    pallas_call x2, Pallas kernels, shards(): call(functools.partial(means_body, peers, fracs), [(table, f32)])  10.1 us
  transfers between devices with their start and end apart: 4, of which 2 were waited for; matrix products, arithmetic and copies ran while one was open for 2% of the time, Pallas kernels for 3%

profile of v1, /device:TPU:0, one launch (start us, length us, event | category | flops | bytes accessed | tf_op | source)
XLA Modules:
  0.0 344.8 jit_solution(14296867855009240475)
XLA Ops:
  0.6 0.7 broadcast_add_fusion
  1.4 0.7 subtract_and_fusion
  2.1 1.0 stack.27.record_ref
  3.1 2.6 shard_map.122
  5.6 7.3 %all-to-all-start.1 = ((s32[32,1,128]{2,1,0:T(1,128)}), s32[32,1,128]{2,1,0:T(1,128)S(1)}, u32[]{:S(2)}, u32[]{:S(2)}) async-start(s32[32,1,128]{2,1,0:T(1,128)} %bitcast.11), calls=%async_computation.1 | async-start | bytes 32768 | tf_op jit(solution)/shard_map/all_to_all | solution.py:290
  12.9 0.8 dynamic_slice.3
  13.7 1.6 copy-done
  15.3 11.1 %shard_map.123 = (f32[256,256]{1,0:T(8,128)S(1)}, f32[32,64,128]{2,1,0:T(8,128)}, f32[32,128]{1,0:T(8,128)S(1)}) custom-call(f32[4096,128]{1,0:T(8,128)S(1)} %bitcast.45, s32[32,128]{1,0:T(8,128)S(1)} %get-tuple-element.14.sender_ref), custom_call_target="tpu_custom_call" | custom-call | tf_op jit(solution)/shard_map/pallas_call | solution.py:342
  26.4 5.3 %shard_map.124 = f32[32,128]{1,0:T(8,128)} custom-call(f32[256,256]{1,0:T(8,128)S(1)} %get-tuple-element.17.edges_ref, s32[32,128]{1,0:T(8,128)S(1)} %bitcast.46), custom_call_target="tpu_custom_call" | custom-call | tf_op jit(solution)/shard_map/pallas_call | solution.py:348
  31.8 5.8 %all-to-all-start.2 = ((f32[32,1,128]{2,1,0:T(1,128)}), f32[32,1,128]{2,1,0:T(1,128)S(1)}, u32[]{:S(2)}, u32[]{:S(2)}) async-start(f32[32,1,128]{2,1,0:T(1,128)} %bitcast.14), calls=%async_computation.2 | async-start | bytes 32768 | tf_op jit(solution)/shard_map/all_to_all | solution.py:290
  37.6 7.0 %all-to-all-done.2 = f32[32,1,128]{2,1,0:T(1,128)S(1)} async-done(((f32[32,1,128]{2,1,0:T(1,128)}), f32[32,1,128]{2,1,0:T(1,128)S(1)}, u32[]{:S(2)}, u32[]{:S(2)}) %all-to-all-start.2) | async-done | bytes 16416 | tf_op jit(solution)/shard_map/all_to_all | solution.py:290
  44.6 13.2 %shard_map.125 = (f32[8,128]{1,0:T(8,128)}, f32[32,128]{1,0:T(8,128)S(1)}) custom-call(f32[32,128]{1,0:T(8,128)S(1)} %get-tuple-element.16.mean_ref, f32[32,128]{1,0:T(8,128)S(1)} %bitcast.53, s32[32,128]{1,0:T(8,128)S(1)} %get-tuple-element.19.index_ref, f32[8,128]{1,0:T(8,128)S(1)} %pad_bitcast_fusion.weight_ref), custom_call_target="tpu_custom_call" | custom-call | tf_op jit(solution)/shard_map/pallas_call | solution.py:349
  57.9 9.3 %all_to_all.65 = f32[32,1,128]{2,1,0:T(1,128)} all-to-all(f32[32,1,128]{2,1,0:T(1,128)S(1)} %bitcast.56), channel_id=1, replica_groups=mesh['gx'=4,'gy'=8] {'gx','gy'}, dimensions={0} | all-to-all | bytes 32768 | tf_op jit(solution)/shard_map/all_to_all | solution.py:290
  67.2 2.6 all-to-all-start
  70.0 27.4 %all-to-all-done.rows_ref = f32[32,64,128]{2,1,0:T(8,128)S(1)} async-done(((f32[32,64,128]{2,1,0:T(8,128)}), f32[32,64,128]{2,1,0:T(8,128)S(1)}, u32[]{:S(2)}, u32[]{:S(2)}) %all-to-all-start) | async-done | bytes 1048608 | tf_op jit(solution)/shard_map/all_to_all | solution.py:290
  97.4 1.0 copy-done.2
  98.4 1.2 copy-done.3
  99.6 0.7 copy-done.8
  100.3 50.2 %shard_map.126.fields_ref = f32[4096,128]{1,0:T(8,128)S(1)} custom-call(f32[32,64,128]{2,1,0:T(8,128)S(1)} %copy-done.3, f32[32,128]{1,0:T(8,128)S(1)} %bitcast.51, s32[32,128]{1,0:T(8,128)S(1)} %bitcast.47, f32[256,256]{1,0:T(8,128)S(1)} %get-tuple-element.17.edges_ref, f32[4096,128]{1,0:T(8,128)} %bitcast.44, f32[256,1024]{1,0:T(8,128)S(1)} %copy-done.1, ...), custom_call_target="tpu_custom_call" | custom-call | tf_op jit(solution)/shard_map/pallas_call | solution.py:352
  150.6 10.1 %shard_map.127 = (f32[256,256]{1,0:T(8,128)S(1)}, f32[32,64,128]{2,1,0:T(8,128)S(1)}, f32[32,128]{1,0:T(8,128)S(1)}) custom-call(f32[4096,128]{1,0:T(8,128)S(1)} %shard_map.126.fields_ref, s32[32,128]{1,0:T(8,128)S(1)} %copy-done.6), custom_call_target="tpu_custom_call" | custom-call | tf_op jit(solution)/shard_map/pallas_call | solution.py:342
  160.7 1.0 copy-done.4
  161.7 4.7 %shard_map.128 = f32[32,128]{1,0:T(8,128)S(1)} custom-call(f32[256,256]{1,0:T(8,128)S(1)} %get-tuple-element.23.edges_ref, s32[32,128]{1,0:T(8,128)S(1)} %bitcast.48), custom_call_target="tpu_custom_call" | custom-call | tf_op jit(solution)/shard_map/pallas_call | solution.py:348
  166.4 9.4 %all_to_all.66 = f32[32,1,128]{2,1,0:T(1,128)S(1)} all-to-all(f32[32,1,128]{2,1,0:T(1,128)S(1)} %bitcast.52), channel_id=1, replica_groups=mesh['gx'=4,'gy'=8] {'gx','gy'}, dimensions={0} | all-to-all | bytes 32768 | tf_op jit(solution)/shard_map/all_to_all | solution.py:290
  175.8 12.8 %shard_map.129 = (f32[8,128]{1,0:T(8,128)S(1)}, f32[32,128]{1,0:T(8,128)S(1)}) custom-call(f32[32,128]{1,0:T(8,128)S(1)} %get-tuple-element.22.mean_ref, f32[32,128]{1,0:T(8,128)S(1)} %bitcast.54, s32[32,128]{1,0:T(8,128)S(1)} %copy-done.10, f32[8,128]{1,0:T(8,128)S(1)} %copy-done.12), custom_call_target="tpu_custom_call" | custom-call | tf_op jit(solution)/shard_map/pallas_call | solution.py:349
  188.6 9.3 %all_to_all.67 = f32[32,1,128]{2,1,0:T(1,128)} all-to-all(f32[32,1,128]{2,1,0:T(1,128)S(1)} %bitcast.55), channel_id=1, replica_groups=mesh['gx'=4,'gy'=8] {'gx','gy'}, dimensions={0} | all-to-all | bytes 32768 | tf_op jit(solution)/shard_map/all_to_all | solution.py:290
  197.9 3.4 all-to-all-start.4
  201.3 86.8 %all_gather.3 = f32[256,128]{1,0:T(8,128)} all-gather(f32[8,128]{1,0:T(8,128)} %copy-done.13), channel_id=1, replica_groups=mesh['gx'=4,'gy'=8] {'gx','gy'}, dimensions={0}, use_global_device_ids=true | all-gather | bytes 135168 | tf_op jit(solution)/shard_map/all_gather | solution.py:362
  288.1 1.6 reshape.48
  289.6 1.5 slice.4
  291.2 1.7 reshape.49
  292.8 0.7 copy-done.7
  293.6 51.2 %shard_map.130 = f32[4096,128]{1,0:T(8,128)} custom-call(f32[32,64,128]{2,1,0:T(8,128)} %all-to-all-done.4.rows_ref, f32[32,128]{1,0:T(8,128)S(1)} %bitcast.50, s32[32,128]{1,0:T(8,128)S(1)} %bitcast.49, f32[256,256]{1,0:T(8,128)S(1)} %get-tuple-element.23.edges_ref, f32[4096,128]{1,0:T(8,128)S(1)} %shard_map.126.fields_ref, f32[256,1024]{1,0:T(8,128)S(1)} %copy-done.1, ...), custom_call_target="tpu_custom_call" | custom-call | tf_op jit(solution)/shard_map/pallas_call | solution.py:352
  (29 shorter events, 0.2 us)
Async XLA Ops:
  5.6 20.8 %copy-start.5 = (s32[32,128]{1,0:T(8,128)}, s32[32,128]{1,0:T(8,128)S(1)}, u32[]{:S(2)}) copy-start(s32[32,128]{1,0:T(8,128)S(1)} %get-tuple-element.14.sender_ref) | copy-start | bytes 49156
  5.6 61.5 %copy-start.9 = (s32[32,128]{1,0:T(8,128)}, s32[32,128]{1,0:T(8,128)S(1)}, u32[]{:S(2)}) copy-start(s32[32,128]{1,0:T(8,128)S(1)} %get-tuple-element.19.index_ref) | copy-start | bytes 49156
  5.6 20.8 %all-to-all-start.1 = ((s32[32,1,128]{2,1,0:T(1,128)}), s32[32,1,128]{2,1,0:T(1,128)S(1)}, u32[]{:S(2)}, u32[]{:S(2)}) async-start(s32[32,1,128]{2,1,0:T(1,128)} %bitcast.11), calls=%async_computation.1 | async-start | bytes 32768 | tf_op jit(solution)/shard_map/all_to_all | solution.py:290
  13.7 1.6 copy-start
  15.3 54.5 %copy-start.14 = (f32[256,2]{0,1:T(2,128)S(1)}, f32[256,2]{0,1:T(2,128)}, u32[]{:S(2)}) copy-start(f32[256,2]{0,1:T(2,128)} %param.14) | copy-start | bytes 6148
  15.3 83.1 %copy-start.1 = (f32[256,1024]{1,0:T(8,128)S(1)}, f32[256,1024]{1,0:T(8,128)}, u32[]{:S(2)}) copy-start(f32[256,1024]{1,0:T(8,128)} %aperture_ref.3) | copy-start | bytes 3145732
  31.8 12.9 %all-to-all-start.2 = ((f32[32,1,128]{2,1,0:T(1,128)}), f32[32,1,128]{2,1,0:T(1,128)S(1)}, u32[]{:S(2)}, u32[]{:S(2)}) async-start(f32[32,1,128]{2,1,0:T(1,128)} %bitcast.14), calls=%async_computation.2 | async-start | bytes 32768 | tf_op jit(solution)/shard_map/all_to_all | solution.py:290
  37.6 29.6 %copy-start.11 = (f32[8,128]{1,0:T(8,128)}, f32[8,128]{1,0:T(8,128)S(1)}, u32[]{:S(2)}) copy-start(f32[8,128]{1,0:T(8,128)S(1)} %pad_bitcast_fusion.weight_ref) | copy-start | bytes 12292
  67.2 30.2 %all-to-all-start = ((f32[32,64,128]{2,1,0:T(8,128)}), f32[32,64,128]{2,1,0:T(8,128)S(1)}, u32[]{:S(2)}, u32[]{:S(2)}) async-start(f32[32,64,128]{2,1,0:T(8,128)} %get-tuple-element.15), calls=%async_computation | async-start | bytes 2097152 | tf_op jit(solution)/shard_map/all_to_all | solution.py:290
  97.4 1.0 copy-start.2
  98.4 1.2 copy-start.3
  99.6 0.7 copy-start.8
  100.3 50.2 %copy-start.6 = (s32[32,128]{1,0:T(8,128)S(1)}, s32[32,128]{1,0:T(8,128)}, u32[]{:S(2)}) copy-start(s32[32,128]{1,0:T(8,128)} %copy-done.5) | copy-start | bytes 49156
  150.6 25.2 %copy-start.10 = (s32[32,128]{1,0:T(8,128)S(1)}, s32[32,128]{1,0:T(8,128)}, u32[]{:S(2)}) copy-start(s32[32,128]{1,0:T(8,128)} %copy-done.9) | copy-start | bytes 49156
  150.6 25.2 %copy-start.12 = (f32[8,128]{1,0:T(8,128)S(1)}, f32[8,128]{1,0:T(8,128)}, u32[]{:S(2)}) copy-start(f32[8,128]{1,0:T(8,128)} %copy-done.11) | copy-start | bytes 12292
  160.7 1.0 copy-start.4
  188.6 9.3 %copy-start.13 = (f32[8,128]{1,0:T(8,128)}, f32[8,128]{1,0:T(8,128)S(1)}, u32[]{:S(2)}) copy-start(f32[8,128]{1,0:T(8,128)S(1)} %get-tuple-element.25) | copy-start | bytes 12292
  197.9 95.0 %all-to-all-start.4 = ((f32[32,64,128]{2,1,0:T(8,128)}), f32[32,64,128]{2,1,0:T(8,128)}, u32[]{:S(2)}, u32[]{:S(2)}) async-start(f32[32,64,128]{2,1,0:T(8,128)} %copy-done.4), calls=%async_computation.4 | async-start | bytes 2097152 | tf_op jit(solution)/shard_map/all_to_all | solution.py:290
  292.8 0.7 copy-start.7

commit v2 on v1

--- a/solution.py
+++ b/solution.py
@@ -13,6 +13,7 @@
 SLOT = 128
 LANES = 128
 TILES = GRID * GRID // LANES
+GROUP = 8
 AXES = ("gx", "gy")
 NT = (((1,), (1,)), ((), ()))
 NN = (((1,), (0,)), ((), ()))
@@ -20,12 +21,6 @@
 
 def dot(a, b, dims):
     return lax.dot_general(a, b, dims, preferred_element_type=jnp.float32)
-
-
-def dot_exact(a, b, dims):
-    return lax.dot_general(
-        a, b, dims, precision=lax.Precision.HIGHEST, preferred_element_type=jnp.float32
-    )
 
 
 def split3(x):
@@ -97,73 +92,162 @@
             start = i * 8 * GRID + c * 4 * GRID
             split_ref[start : start + 4 * GRID, :] = part
 
-    def one_peer(d, carry):
-        edge, frac = edge_and_frac(sender_ref[pl.ds(d, 1), :], fracs)
-        onehot = equal(iota((fracs, SLOT), 0), frac)
+    def one_pair(d):
+        codes = jnp.concatenate([sender_ref[pl.ds(d + i, 1), :] for i in range(2)], 1)
+        edge, frac = edge_and_frac(codes, fracs)
+        onehot = equal(iota((fracs, 2 * SLOT), 0), frac)
         picked = dot(split_ref[...], onehot, NN)
         picked = picked[: 8 * GRID] + picked[8 * GRID : 16 * GRID] + picked[16 * GRID :]
         for c in range(2):
-            row = jnp.zeros((GRID, SLOT), jnp.float32)
+            row = jnp.zeros((GRID, 2 * SLOT), jnp.float32)
             for e in range(4):
                 start = c * 4 * GRID + e * GRID
                 row = jnp.where(edge == e, picked[start : start + GRID], row)
-            rows_ref[d, c * GRID : (c + 1) * GRID, :] = row
-            if c == 0:
-                mean_ref[pl.ds(d, 1), :] = jnp.sum(row, 0, keepdims=True) * (1.0 / GRID)
-        return carry
-
-    lax.fori_loop(0, peers, one_peer, 0)
-
-
-def means_body(peers, fracs, edges_ref, arrived_ref, mean_ref):
+            for i in range(2):
+                half = row[:, i * SLOT : (i + 1) * SLOT]
+                rows_ref[d + i, c * GRID : (c + 1) * GRID, :] = half
+                if c == 0:
+                    mean = jnp.sum(half, 0, keepdims=True) * (1.0 / GRID)
+                    mean_ref[pl.ds(d + i, 1), :] = mean
+
+    def pairs(g, carry):
+        one_pair(g * 4)
+        one_pair(g * 4 + 2)
+        return carry
+
+    lax.fori_loop(0, peers // 4, pairs, 0)
+
+
+def lanes_of(ref, start, rows=None):
+    if rows is None:
+        return jnp.concatenate([ref[pl.ds(start + i, 1), :] for i in range(GROUP)], 1)
+    return jnp.concatenate([ref[start + i, rows] for i in range(GROUP)], 1)
+
+
+def stacked3(x):
+    parts = [p.astype(jnp.float32) for p in split3(x)] + [jnp.zeros_like(x)]
+    return jnp.concatenate(parts, 0).astype(jnp.bfloat16)
+
+
+def sum3(x):
+    return x[:8] + x[8:16] + x[16:24]
+
+
+def traffic_body(
+    peers,
+    columns,
+    fracs,
+    high,
+    rows_ref,
+    mean_ref,
+    edges_ref,
+    arrived_ref,
+    index_ref,
+    weight_ref,
+    rows_out,
+    extra_out,
+    own_send,
+    own_recv,
+    extra_send,
+    send_sem,
+    recv_sem,
+):
+    me = lax.axis_index(AXES[0]) * columns + lax.axis_index(AXES[1])
+
+    def device(step):
+        target = lax.rem(me + step, peers)
+        return target, (target // columns, lax.rem(target, columns))
+
+    barrier = pltpu.get_barrier_semaphore()
+
+    def greet(step, carry):
+        pl.semaphore_signal(
+            barrier, inc=1, device_id=device(step)[1], device_id_type=pl.DeviceIdType.MESH
+        )
+        return carry
+
+    lax.fori_loop(1, peers, greet, 0)
+    pl.semaphore_wait(barrier, peers - 1)
+
+    def send_all(source, target, kind):
+        def one(step, carry):
+            there, device_id = device(step)
+            pltpu.make_async_remote_copy(
+                src_ref=source.at[there],
+                dst_ref=target.at[me],
+                send_sem=send_sem.at[kind],
+                recv_sem=recv_sem.at[kind],
+                device_id=device_id,
+                device_id_type=pl.DeviceIdType.MESH,
+            ).start()
+            return carry
+
+        lax.fori_loop(1, peers, one, 0)
+        target[me] = source[me]
+
+    def wait_all(ref, sem):
+        others = ref.at[pl.ds(0, peers - 1)]
+        pltpu.make_async_copy(others, others, sem).wait()
+
+    send_all(rows_ref, rows_out, 0)
+
     means = [
         jnp.sum(edges_ref[e * GRID : (e + 1) * GRID, :], 0, keepdims=True) * (1.0 / GRID)
         for e in range(4)
     ]
-    table = jnp.concatenate(means + means, 0)
-    parts = jnp.concatenate(
-        [p.astype(jnp.float32) for p in split3(table)] + [jnp.zeros_like(table)], 0
-    ).astype(jnp.bfloat16)
-
-    def one_peer(d, carry):
-        edge, frac = edge_and_frac(arrived_ref[pl.ds(d, 1), :], fracs)
-        picked = dot(parts, equal(iota((fracs, SLOT), 0), frac), NN)
-        picked = picked[:8] + picked[8:16] + picked[16:24]
-        mine = jnp.where(iota((8, SLOT), 0) == edge, picked, 0.0)
-        mean_ref[pl.ds(d, 1), :] = jnp.sum(mine, 0, keepdims=True)
-        return carry
-
-    lax.fori_loop(0, peers, one_peer, 0)
-
-
-def coarse_body(peers, high, mean_ref, other_ref, index_ref, weight_ref, corr_ref, out_ref):
-    def tables(d):
-        index = index_ref[pl.ds(d, 1), :]
+    parts = stacked3(jnp.concatenate(means + means, 0))
+    wide = GROUP * SLOT
+
+    def own_means(g, carry):
+        edge, frac = edge_and_frac(lanes_of(arrived_ref, g * GROUP), fracs)
+        picked = sum3(dot(parts, equal(iota((fracs, wide), 0), frac), NN))
+        mine = jnp.sum(jnp.where(iota((8, wide), 0) == edge, picked, 0.0), 0, keepdims=True)
+        for i in range(GROUP):
+            own_send[g * GROUP + i] = mine[:, i * SLOT : (i + 1) * SLOT]
+        return carry
+
+    lax.fori_loop(0, peers // GROUP, own_means, 0)
+    send_all(own_send, own_recv, 1)
+    wait_all(own_recv, recv_sem.at[1])
+
+    def tables(g):
+        index = lanes_of(index_ref, g * GROUP)
         row = jnp.where(index >= 0, index >> 7, -1)
         lane = jnp.where(index >= 0, index & (LANES - 1), -1)
-        return iota((high, SLOT), 0) == row, equal(iota((LANES, SLOT), 0), lane, jnp.float32)
-
-    def collect(d, total):
-        rows, lanes = tables(d)
-        mismatch = mean_ref[pl.ds(d, 1), :] - other_ref[pl.ds(d, 1), :]
-        return total + dot_exact(jnp.where(rows, mismatch, 0.0), lanes, NT)
-
-    residual = lax.fori_loop(0, peers, collect, jnp.zeros((high, LANES), jnp.float32))
-    correction = residual * weight_ref[...]
-    corr_ref[...] = correction
-
-    def pick(d, carry):
-        rows, lanes = tables(d)
-        picked = dot_exact(correction, lanes, NN)
-        out_ref[pl.ds(d, 1), :] = jnp.sum(jnp.where(rows, picked, 0.0), 0, keepdims=True)
-        return carry
-
-    lax.fori_loop(0, peers, pick, 0)
+        return iota((8, wide), 0) == row, equal(iota((LANES, wide), 0), lane)
+
+    def collect(g, total):
+        rows, onehot = tables(g)
+        other = jnp.concatenate([own_recv[g * GROUP + i] for i in range(GROUP)], 1)
+        mismatch = lanes_of(mean_ref, g * GROUP) - other
+        return total + dot(stacked3(jnp.where(rows, mismatch, 0.0)), onehot, NT)
+
+    residual = lax.fori_loop(0, peers // GROUP, collect, jnp.zeros((32, LANES), jnp.float32))
+    correction = sum3(residual) * weight_ref[...]
+    halves = stacked3(correction)
+
+    def pick(g, carry):
+        rows, onehot = tables(g)
+        picked = jnp.where(rows, sum3(dot(halves, onehot, NN)), 0.0)
+        mine = jnp.sum(picked, 0, keepdims=True)
+        for i in range(GROUP):
+            extra_send[g * GROUP + i] = jnp.where(
+                iota((8, SLOT), 0) == high, mine[:, i * SLOT : (i + 1) * SLOT], correction
+            )
+        return carry
+
+    lax.fori_loop(0, peers // GROUP, pick, 0)
+    send_all(extra_send, extra_out, 2)
+    wait_all(extra_out, recv_sem.at[2])
+    wait_all(rows_out, recv_sem.at[0])
+    for kind, ref in ((0, rows_out), (1, own_recv), (2, extra_out)):
+        wait_all(ref, send_sem.at[kind])
 
 
 def sweep_body(
     peers,
     fracs,
+    high,
     rows_ref,
     extra_ref,
     arrived_ref,
@@ -181,28 +265,31 @@
     sum_ref[...] = jnp.zeros_like(sum_ref)
     count_ref[...] = jnp.zeros_like(count_ref)
 
-    def one_peer(d, carry):
-        edge, frac = edge_and_frac(arrived_ref[pl.ds(d, 1), :], fracs)
-        onehot = equal(iota((fracs, SLOT), 0), frac)
-        values = rows_ref[d] + extra_ref[pl.ds(d, 1), :]
+    wide = GROUP * SLOT
+
+    def one_group(g, carry):
+        edge, frac = edge_and_frac(lanes_of(arrived_ref, g * GROUP), fracs)
+        onehot = equal(iota((fracs, wide), 0), frac)
+        extra = lanes_of(extra_ref, g * GROUP, slice(high, high + 1))
+        values = lanes_of(rows_ref, g * GROUP, slice(0, 2 * GRID)) + extra
         masked = []
         for c in range(2):
             for e in range(4):
                 masked.append(jnp.where(edge == e, values[c * GRID : (c + 1) * GRID], 0.0))
-        masked = jnp.concatenate(masked, 0)
-        total = sum_ref[...]
-        for part in split3(masked):
-            total = total + dot(part, onehot, NT)
-        sum_ref[...] = total
-        count_ref[...] += dot(equal(iota((16, SLOT), 0), edge), onehot, NT)
-        return carry
-
-    lax.fori_loop(0, peers, one_peer, 0)
+        parts = split3(jnp.concatenate(masked, 0))
+        sum_ref[...] += dot(jnp.concatenate(parts, 0), onehot, NT)
+        count_ref[...] += dot(equal(iota((16, wide), 0), edge), onehot, NT)
+        return carry
+
+    lax.fori_loop(0, peers // GROUP, one_group, 0)
     for c in range(2):
         borders = []
         for e in range(4):
             start = (c * 4 + e) * GRID
-            total = edges_ref[start : start + GRID, :] + sum_ref[start : start + GRID, :]
+            total = edges_ref[start : start + GRID, :]
+            for i in range(3):
+                part = start + i * 8 * GRID
+                total = total + sum_ref[part : part + GRID, :]
             borders.append(total / (1.0 + count_ref[e : e + 1, :]))
         border = jnp.transpose(jnp.concatenate(borders, 0))
         border_ref[c] = border
@@ -239,6 +326,7 @@
         w_down = [0.5 * (a[t] + below[t]) for t in range(TILES)]
         w_left = [0.5 * (a[t] + jnp.where(west_end, a[t], left[t])) for t in range(TILES)]
         w_right = [0.5 * (a[t] + jnp.where(east_end, a[t], right[t])) for t in range(TILES)]
+        fields = []
         for c in range(2):
             store = storage_ref[here, c : c + 1]
             border = border_ref[c, here, :]
@@ -262,27 +350,32 @@
                 cd.append(down)
                 cl.append(jnp.where(west_end, 0.0, w_left[t] * inverse))
                 cr.append(jnp.where(east_end, 0.0, w_right[t] * inverse))
-            for sweep in range(SWEEPS):
-                above, below, left, right = neighbours(x)
-                x = [
+            fields.append((x, s, cu, cd, cl, cr))
+        state = [f[0] for f in fields]
+        for sweep in range(SWEEPS):
+            for c in range(2):
+                above, below, left, right = neighbours(state[c])
+                _, s, cu, cd, cl, cr = fields[c]
+                state[c] = [
                     (s[t] + cu[t] * above[t])
                     + (cd[t] * below[t] + (cl[t] * left[t] + cr[t] * right[t]))
                     for t in range(TILES)
                 ]
+        for c in range(2):
             for t in range(TILES):
                 at = pl.ds(start * 2 * TILES + t * 2 + c, 8, stride=2 * TILES)
-                out_ref[at, :] = x[t]
+                out_ref[at, :] = state[c][t]
         return carry
 
     lax.fori_loop(0, fracs // 8, one_tile, 0)
 
 
-def call(body, shapes, scratch=()):
+def call(body, shapes, scratch=(), **params):
     return pl.pallas_call(
         body,
         out_shape=[jax.ShapeDtypeStruct(shape, dtype) for shape, dtype in shapes],
         scratch_shapes=list(scratch),
-        compiler_params=pltpu.CompilerParams(vmem_limit_bytes=48 * 1024 * 1024),
+        compiler_params=pltpu.CompilerParams(vmem_limit_bytes=48 * 1024 * 1024, **params),
     )
 
 
@@ -313,7 +406,8 @@
     peers = lax.axis_size(AXES)
     coarse = coarse_weight.shape[0]
     per_dev = coarse // peers
-    high = -(-per_dev // (8 * LANES)) * 8
+    high = -(-per_dev // LANES)
+    columns = lax.axis_size(AXES[1])
     first = lax.axis_index(AXES) * per_dev
     local = coarse_index - first
     none = jnp.zeros_like(local)
@@ -331,7 +425,7 @@
         0,
     )
     weight = lax.dynamic_slice(coarse_weight, (first,), (per_dev,))
-    weight = jnp.pad(weight, (0, high * LANES - per_dev)).reshape(high, LANES)
+    weight = jnp.pad(weight, (0, 8 * LANES - per_dev)).reshape(8, LANES)
     table = (peers, SLOT)
     sender, target, index = call(
         functools.partial(slots_body, peers, fracs), [(table, i32)] * 3
@@ -344,23 +438,30 @@
             [((8 * GRID, fracs), f32), ((peers, 2 * GRID, SLOT), f32), (table, f32)],
             [pltpu.VMEM((24 * GRID, fracs), jnp.bfloat16)],
         )(state, sender)
-        rows = exchange(rows)
-        (own,) = call(functools.partial(means_body, peers, fracs), [(table, f32)])(edges, arrived)
-        correction, extra = call(
-            functools.partial(coarse_body, peers, high), [((high, LANES), f32), (table, f32)]
-        )(mean, exchange(own), index, weight)
+        rows, extra = call(
+            functools.partial(traffic_body, peers, columns, fracs, high),
+            [((peers, 2 * GRID, SLOT), f32), ((peers, 8, LANES), f32)],
+            [
+                pltpu.VMEM((peers, 1, SLOT), f32),
+                pltpu.VMEM((peers, 1, SLOT), f32),
+                pltpu.VMEM((peers, 8, LANES), f32),
+                pltpu.SemaphoreType.DMA((3,)),
+                pltpu.SemaphoreType.DMA((3,)),
+            ],
+            collective_id=0,
+            has_side_effects=True,
+        )(rows, mean, edges, arrived, index, weight)
         (state,) = call(
-            functools.partial(sweep_body, peers, fracs),
+            functools.partial(sweep_body, peers, fracs, high),
             [(state.shape, f32)],
             [
-                pltpu.VMEM((8 * GRID, fracs), f32),
+                pltpu.VMEM((24 * GRID, fracs), f32),
                 pltpu.VMEM((16, fracs), f32),
                 pltpu.VMEM((2, fracs, 4 * GRID), f32),
                 pltpu.VMEM((2, fracs, GRID * GRID), f32),
             ],
-        )(rows, exchange(extra), arrived, edges, state, aperture, sources, storage)
-    blocks = lax.all_gather(correction, AXES, tiled=True)
-    coarse_out = blocks.reshape(peers, high * LANES)[:, :per_dev].reshape(coarse)
+        )(rows, extra, arrived, edges, state, aperture, sources, storage)
+    coarse_out = extra.reshape(peers, 8 * LANES)[:, :per_dev].reshape(coarse)
     fields_out = state.reshape(fracs, TILES, 2, LANES).transpose(0, 2, 1, 3).reshape(fields.shape)
     return fields_out, coarse_out
 

time: 346 us -> 169 us (0.49)
  blocking collectives: 115 us -> 0 us
  waiting for transfers between devices: 34.5 us -> 0.01 us
  starting transfers between devices: 19.2 us -> 7.3 us
  local copies, waits for them, and re-layouts: 12.9 us -> 4.95 us
  Pallas kernels: 161 us -> 154 us
    all_gather x1 -> x0, blocking collectives: 86.8 us -> none  [shards(): blocks = lax.all_gather(correction, AXES, tiled=True)]
    all_to_all x4 -> x1, waiting for transfers between devices: 34.5 us -> 0.01 us  [exchange(): return lax.all_to_all(x, AXES, split_axis=0, concat_axis=0, tiled=True)]
    all_to_all x3 -> x0, blocking collectives: 27.9 us -> none  [exchange(): return lax.all_to_all(x, AXES, split_axis=0, concat_axis=0, tiled=True)]
    pallas_call x2, Pallas kernels: 21.2 us -> 8.79 us  [shards(): call(functools.partial(edges_body, peers, fracs), [((8 * GRID, fracs), f3...]
    all_to_all x4 -> x1, starting transfers between devices: 19.2 us -> 7.3 us  [exchange(): return lax.all_to_all(x, AXES, split_axis=0, concat_axis=0, tiled=True)]
    pallas_call x6 -> x4, Pallas kernels: 138 us -> 143 us  [the longest x2 73.4 us: shards(): call(functools.partial(traffic_body, peers, columns, fracs, high), [((pee...]
    unnamed x31 -> x6, local copies, waits for them, and re-layouts: 6.35 us -> 2.43 us
  transfers between devices with their start and end apart: 4 -> 1, of which waited for: 2 -> 0; matrix products, arithmetic and copies ran while one was open for 2% -> 1% of each run, Pallas kernels for 3% -> 3%
where the time goes in v2:
time: 169 us
  Pallas kernels  154 us (91%)
  starting transfers between devices  7.3 us (4%)
  local copies, waits for them, and re-layouts  4.95 us (3%)
    pallas_call x2, Pallas kernels, shards(): call(functools.partial(traffic_body, peers, columns, fracs, high), [((pee...  73.4 us
    pallas_call x2, Pallas kernels, shards(): call(functools.partial(sweep_body, peers, fracs, high), [(state.shape, f3...  69.7 us
    pallas_call x2, Pallas kernels, shards(): call(functools.partial(edges_body, peers, fracs), [((8 * GRID, fracs), f3...  8.79 us
    all_to_all x1, starting transfers between devices, exchange(): return lax.all_to_all(x, AXES, split_axis=0, concat_axis=0, tiled=True)  7.3 us
  transfers between devices with their start and end apart: 1, of which 0 were waited for; matrix products, arithmetic and copies ran while one was open for 1% of the time, Pallas kernels for 3%

profile of v2, /device:TPU:0, one launch (start us, length us, event | category | flops | bytes accessed | tf_op | source)
XLA Modules:
  0.0 168.9 jit_solution(13231194239131416403)
XLA Ops:
  0.6 0.7 broadcast_add_fusion
  1.4 0.7 subtract_and_fusion
  2.1 1.0 stack.27.record_ref
  3.1 2.6 %shard_map.122 = (s32[32,128]{1,0:T(8,128)S(1)}, s32[32,128]{1,0:T(8,128)}, s32[32,128]{1,0:T(8,128)S(1)}) custom-call(s32[8,4096]{1,0:T(8,128)S(1)} %stack.27.record_ref), custom_call_target="tpu_custom_call" | custom-call | tf_op jit(solution)/shard_map/pallas_call | solution.py:430
  5.6 7.3 %all-to-all-start = ((s32[32,1,128]{2,1,0:T(1,128)}), s32[32,1,128]{2,1,0:T(1,128)S(1)}, u32[]{:S(2)}, u32[]{:S(2)}) async-start(s32[32,1,128]{2,1,0:T(1,128)} %bitcast.11), calls=%async_computation | async-start | bytes 32768 | tf_op jit(solution)/shard_map/all_to_all | solution.py:383
  12.9 0.8 dynamic_slice.3
  13.7 0.8 copy.21.storage_ref
  14.5 0.0 copy-start
  14.6 1.6 copy-done
  16.1 0.0 copy-start.1
  16.1 4.4 %shard_map.123 = (f32[256,256]{1,0:T(8,128)S(1)}, f32[32,64,128]{2,1,0:T(8,128)S(1)}, f32[32,128]{1,0:T(8,128)S(1)}) custom-call(f32[4096,128]{1,0:T(8,128)S(1)} %bitcast.33, s32[32,128]{1,0:T(8,128)S(1)} %get-tuple-element.15.sender_ref), custom_call_target="tpu_custom_call" | custom-call | tf_op jit(solution)/shard_map/pallas_call | solution.py:436
  20.5 0.0 all-to-all-done
  20.6 38.1 %shard_map.124 = (f32[32,64,128]{2,1,0:T(8,128)S(1)}, f32[32,8,128]{2,1,0:T(8,128)S(1)}) custom-call(f32[32,64,128]{2,1,0:T(8,128)S(1)} %get-tuple-element.16.rows_ref, f32[32,128]{1,0:T(8,128)S(1)} %get-tuple-element.17.mean_ref, f32[256,256]{1,0:T(8,128)S(1)} %get-tuple-element.18.edges_ref, s32[32,128]{1,0:T(8,128)S(1)} %bitcast.35, ...), custom_call_target="tpu_custom_call" | custom-call | tf_op jit(solution)/shard_map/pallas_call | solution.py:441
  58.7 0.0 copy-done.1
  58.7 34.5 %shard_map.125.fields_ref = f32[4096,128]{1,0:T(8,128)S(1)} custom-call(f32[32,64,128]{2,1,0:T(8,128)S(1)} %get-tuple-element.21.rows_ref, f32[32,8,128]{2,1,0:T(8,128)S(1)} %get-tuple-element.22.extra_ref, s32[32,128]{1,0:T(8,128)S(1)} %bitcast.36, f32[256,256]{1,0:T(8,128)S(1)} %get-tuple-element.18.edges_ref, f32[4096,128]{1,0:T(8,128)} %bitcast.32, ...), custom_call_target="tpu_custom_call" | custom-call | tf_op jit(solution)/shard_map/pallas_call | solution.py:454
  93.2 4.4 %shard_map.126 = (f32[256,256]{1,0:T(8,128)S(1)}, f32[32,64,128]{2,1,0:T(8,128)S(1)}, f32[32,128]{1,0:T(8,128)S(1)}) custom-call(f32[4096,128]{1,0:T(8,128)S(1)} %shard_map.125.fields_ref, s32[32,128]{1,0:T(8,128)S(1)} %get-tuple-element.15.sender_ref), custom_call_target="tpu_custom_call" | custom-call | tf_op jit(solution)/shard_map/pallas_call | solution.py:436
  97.6 35.3 %shard_map.127 = (f32[32,64,128]{2,1,0:T(8,128)S(1)}, f32[32,8,128]{2,1,0:T(8,128)S(1)}) custom-call(f32[32,64,128]{2,1,0:T(8,128)S(1)} %get-tuple-element.23.rows_ref, f32[32,128]{1,0:T(8,128)S(1)} %get-tuple-element.24.mean_ref, f32[256,256]{1,0:T(8,128)S(1)} %get-tuple-element.25.edges_ref, s32[32,128]{1,0:T(8,128)S(1)} %bitcast.37, ...), custom_call_target="tpu_custom_call" | custom-call | tf_op jit(solution)/shard_map/pallas_call | solution.py:441
  132.9 35.2 %shard_map.128 = f32[4096,128]{1,0:T(8,128)} custom-call(f32[32,64,128]{2,1,0:T(8,128)S(1)} %get-tuple-element.26.rows_ref, f32[32,8,128]{2,1,0:T(8,128)S(1)} %get-tuple-element.27.extra_ref, s32[32,128]{1,0:T(8,128)S(1)} %bitcast.38, f32[256,256]{1,0:T(8,128)S(1)} %get-tuple-element.25.edges_ref, f32[4096,128]{1,0:T(8,128)S(1)} %shard_map.125.fields_ref, ...), custom_call_target="tpu_custom_call" | custom-call | tf_op jit(solution)/shard_map/pallas_call | solution.py:454
  168.1 0.8 reshape.41
  (4 shorter events, 0.1 us)
Async XLA Ops:
  5.6 14.9 %all-to-all-start = ((s32[32,1,128]{2,1,0:T(1,128)}), s32[32,1,128]{2,1,0:T(1,128)S(1)}, u32[]{:S(2)}, u32[]{:S(2)}) async-start(s32[32,1,128]{2,1,0:T(1,128)} %bitcast.11), calls=%async_computation | async-start | bytes 32768 | tf_op jit(solution)/shard_map/all_to_all | solution.py:383
  14.5 1.6 copy-start
  16.1 42.5 %copy-start.1 = (f32[256,1024]{1,0:T(8,128)S(1)}, f32[256,1024]{1,0:T(8,128)}, u32[]{:S(2)}) copy-start(f32[256,1024]{1,0:T(8,128)} %aperture_ref.3) | copy-start | bytes 3145732

commit v3 on v2

--- a/solution.py
+++ b/solution.py
@@ -63,34 +63,49 @@
     coarse_ref[...] = jnp.where(valid, pieces[4] * LANES + pieces[5], -1)
 
 
-def edge_selector(tile):
-    row = iota((4 * GRID, LANES), 0)
-    k, edge = row & (GRID - 1), row >> 5
-    cell = jnp.where(
-        edge == 0,
-        k,
-        jnp.where(edge == 1, GRID * (GRID - 1) + k, k * GRID + (edge - 2) * (GRID - 1)),
-    )
-    return (iota((4 * GRID, LANES), 1) + tile * LANES) == cell
-
-
 def edge_and_frac(code, fracs):
     shift = fracs.bit_length() - 1
     return jnp.where(code >= 0, code >> shift, -1), jnp.where(code >= 0, code & (fracs - 1), -1)
 
 
-def edges_body(peers, fracs, fields_ref, sender_ref, edges_ref, rows_ref, mean_ref, split_ref):
+def take_edges(cells_ref, edges_ref):
+    size = GRID * GRID
     for c in range(2):
-        total = jnp.zeros((4 * GRID, fracs), jnp.float32)
+        views = (
+            pl.ds(c * size, GRID),
+            pl.ds(c * size + size - GRID, GRID),
+            pl.ds(c * size, GRID, stride=GRID),
+            pl.ds(c * size + GRID - 1, GRID, stride=GRID),
+        )
+        for g in range(cells_ref.shape[0]):
+            lanes = slice(g * LANES, (g + 1) * LANES)
+            for e in range(4):
+                start = (c * 4 + e) * GRID
+                edges_ref[start : start + GRID, lanes] = cells_ref[g, views[e], :]
+
+
+def tile_rows(g, tile, c):
+    return pl.ds(g * LANES * 2 * TILES + tile * 2 + c, LANES, stride=2 * TILES)
+
+
+def turn_body(fields_ref, source_ref, aperture_ref, cells_ref, sources_ref, openings_ref, edges_ref):
+    for g in range(aperture_ref.shape[0] // LANES):
+        lanes = slice(g * LANES, (g + 1) * LANES)
         for tile in range(TILES):
-            cells = fields_ref[pl.ds(tile * 2 + c, fracs, stride=2 * TILES), :]
-            selector = edge_selector(tile).astype(jnp.float32).astype(jnp.bfloat16)
-            for part in split3(cells):
-                total = total + dot(selector, part, NT)
-        edges_ref[c * 4 * GRID : (c + 1) * 4 * GRID, :] = total
-        for i, part in enumerate(split3(total)):
-            start = i * 8 * GRID + c * 4 * GRID
-            split_ref[start : start + 4 * GRID, :] = part
+            there = slice(tile * LANES, (tile + 1) * LANES)
+            openings_ref[g, there, :] = jnp.transpose(aperture_ref[lanes, there])
+            for c in range(2):
+                row = c * GRID * GRID + tile * LANES
+                cells = jnp.transpose(fields_ref[tile_rows(g, tile, c), :])
+                cells_ref[g, row : row + LANES, :] = cells
+                cells = jnp.transpose(source_ref[tile_rows(g, tile, c), :])
+                sources_ref[g, row : row + LANES, :] = cells
+    take_edges(cells_ref, edges_ref)
+
+
+def gather_body(peers, fracs, edges_ref, sender_ref, rows_ref, mean_ref, split_ref):
+    for i, part in enumerate(split3(edges_ref[...])):
+        split_ref[i * 8 * GRID : (i + 1) * 8 * GRID, :] = part
 
     def one_pair(d):
         codes = jnp.concatenate([sender_ref[pl.ds(d + i, 1), :] for i in range(2)], 1)
@@ -169,7 +184,7 @@
     lax.fori_loop(1, peers, greet, 0)
     pl.semaphore_wait(barrier, peers - 1)
 
-    def send_all(source, target, kind):
+    def send_some(source, target, kind, begin, end):
         def one(step, carry):
             there, device_id = device(step)
             pltpu.make_async_remote_copy(
@@ -182,14 +197,15 @@
             ).start()
             return carry
 
-        lax.fori_loop(1, peers, one, 0)
+        lax.fori_loop(begin, end, one, 0)
+
+    def send_all(source, target, kind):
+        send_some(source, target, kind, 1, peers)
         target[me] = source[me]
 
     def wait_all(ref, sem):
         others = ref.at[pl.ds(0, peers - 1)]
         pltpu.make_async_copy(others, others, sem).wait()
-
-    send_all(rows_ref, rows_out, 0)
 
     means = [
         jnp.sum(edges_ref[e * GRID : (e + 1) * GRID, :], 0, keepdims=True) * (1.0 / GRID)
@@ -208,6 +224,8 @@
 
     lax.fori_loop(0, peers // GROUP, own_means, 0)
     send_all(own_send, own_recv, 1)
+    early = peers // 3
+    send_some(rows_ref, rows_out, 0, 1, early)
     wait_all(own_recv, recv_sem.at[1])
 
     def tables(g):
@@ -238,6 +256,8 @@
 
     lax.fori_loop(0, peers // GROUP, pick, 0)
     send_all(extra_send, extra_out, 2)
+    send_some(rows_ref, rows_out, 0, early, peers)
+    rows_out[me] = rows_ref[me]
     wait_all(extra_out, recv_sem.at[2])
     wait_all(rows_out, recv_sem.at[0])
     for kind, ref in ((0, rows_out), (1, own_recv), (2, extra_out)):
@@ -248,20 +268,24 @@
     peers,
     fracs,
     high,
+    last,
     rows_ref,
     extra_ref,
     arrived_ref,
     edges_ref,
-    fields_ref,
-    aperture_ref,
-    source_ref,
+    cells_ref,
+    openings_ref,
+    sources_ref,
     storage_ref,
-    out_ref,
-    sum_ref,
-    count_ref,
-    border_ref,
-    side_ref,
+    *refs,
 ):
+    if last:
+        (out_ref,), scratch = refs[:1], refs[1:]
+        new_ref, scratch = scratch[-1], scratch[:-1]
+    else:
+        (new_ref, new_edges_ref), scratch = refs[:2], refs[2:]
+    sum_ref, count_ref, border_ref, open_ref, even_ref, odd_ref, s_ref = scratch[:7]
+    up_ref, down_ref, left_ref, right_ref = scratch[7:]
     sum_ref[...] = jnp.zeros_like(sum_ref)
     count_ref[...] = jnp.zeros_like(count_ref)
 
@@ -283,91 +307,102 @@
 
     lax.fori_loop(0, peers // GROUP, one_group, 0)
     for c in range(2):
-        borders = []
         for e in range(4):
             start = (c * 4 + e) * GRID
             total = edges_ref[start : start + GRID, :]
             for i in range(3):
                 part = start + i * 8 * GRID
                 total = total + sum_ref[part : part + GRID, :]
-            borders.append(total / (1.0 + count_ref[e : e + 1, :]))
-        border = jnp.transpose(jnp.concatenate(borders, 0))
-        border_ref[c] = border
-        parts = split3(border)
-        for tile in range(TILES):
-            row = iota((4 * GRID, LANES), 0)
-            inject = edge_selector(tile) & (row >= 2 * GRID)
-            inject = inject.astype(jnp.float32).astype(jnp.bfloat16)
-            side = dot(parts[0], inject, NN) + dot(parts[1], inject, NN) + dot(parts[2], inject, NN)
-            side_ref[c, :, tile * LANES : (tile + 1) * LANES] = side
-
-    lane = iota((8, LANES), 1)
-    column = lane & (GRID - 1)
-    first, last = lane < GRID, lane >= LANES - GRID
-    west_end, east_end = column == 0, column == GRID - 1
-
-    def neighbours(x):
-        down = [pltpu.roll(v, GRID, 1) for v in x]
-        up = [pltpu.roll(v, LANES - GRID, 1) for v in x]
-        above = [down[0]] + [jnp.where(first, down[t - 1], down[t]) for t in range(1, TILES)]
-        below = [jnp.where(last, up[t + 1], up[t]) for t in range(TILES - 1)] + [up[-1]]
-        left = [pltpu.roll(v, 1, 1) for v in x]
-        right = [pltpu.roll(v, LANES - 1, 1) for v in x]
-        return above, below, left, right
-
-    def one_tile(i, carry):
-        start = pl.multiple_of(i * 8, 8)
-        here = pl.ds(start, 8)
-        a = [aperture_ref[here, t * LANES : (t + 1) * LANES] for t in range(TILES)]
-        above, below, left, right = neighbours(a)
-        above[0] = jnp.where(first, a[0], above[0])
-        below[-1] = jnp.where(last, a[-1], below[-1])
-        w_up = [0.5 * (a[t] + above[t]) for t in range(TILES)]
-        w_down = [0.5 * (a[t] + below[t]) for t in range(TILES)]
-        w_left = [0.5 * (a[t] + jnp.where(west_end, a[t], left[t])) for t in range(TILES)]
-        w_right = [0.5 * (a[t] + jnp.where(east_end, a[t], right[t])) for t in range(TILES)]
-        fields = []
-        for c in range(2):
-            store = storage_ref[here, c : c + 1]
-            border = border_ref[c, here, :]
-            x, s, cu, cd, cl, cr = [], [], [], [], [], []
-            for t in range(TILES):
-                at = pl.ds(start * 2 * TILES + t * 2 + c, 8, stride=2 * TILES)
-                inverse = 1.0 / (store + w_up[t] + w_down[t] + w_left[t] + w_right[t])
-                side = side_ref[c, here, t * LANES : (t + 1) * LANES]
-                value = source_ref[at, :] + side * jnp.where(west_end, w_left[t], w_right[t])
-                up, down = w_up[t] * inverse, w_down[t] * inverse
-                if t == 0:
-                    value = value + jnp.where(first, border * w_up[t], 0.0)
-                    up = jnp.where(first, 0.0, up)
-                if t == TILES - 1:
-                    bottom = pltpu.roll(border, 2 * GRID, 1)
-                    value = value + jnp.where(last, bottom * w_down[t], 0.0)
-                    down = jnp.where(last, 0.0, down)
-                x.append(fields_ref[at, :])
-                s.append(value * inverse)
-                cu.append(up)
-                cd.append(down)
-                cl.append(jnp.where(west_end, 0.0, w_left[t] * inverse))
-                cr.append(jnp.where(east_end, 0.0, w_right[t] * inverse))
-            fields.append((x, s, cu, cd, cl, cr))
-        state = [f[0] for f in fields]
-        for sweep in range(SWEEPS):
-            for c in range(2):
-                above, below, left, right = neighbours(state[c])
-                _, s, cu, cd, cl, cr = fields[c]
-                state[c] = [
-                    (s[t] + cu[t] * above[t])
-                    + (cd[t] * below[t] + (cl[t] * left[t] + cr[t] * right[t]))
-                    for t in range(TILES)
-                ]
-        for c in range(2):
-            for t in range(TILES):
-                at = pl.ds(start * 2 * TILES + t * 2 + c, 8, stride=2 * TILES)
-                out_ref[at, :] = state[c][t]
+            total = total / (1.0 + count_ref[e : e + 1, :])
+            for g in range(fracs // LANES):
+                border_ref[g, start : start + GRID, :] = total[:, g * LANES : (g + 1) * LANES]
+
+    size = GRID * GRID
+    sublane = iota((8, LANES), 0)
+    top, bottom = sublane == 0, sublane == TILES - 1
+    groups = fracs // LANES
+
+    def fill_ends(ref, start, count):
+        for j in range(start, start + count):
+            if j < GRID:
+                ref[GRID + LANES + j] = pltpu.roll(ref[GRID + j], TILES - 1, 0)
+            if j >= LANES - GRID:
+                ref[j - (LANES - GRID)] = pltpu.roll(ref[GRID + j], 1, 0)
+
+    def one_block(i, carry):
+        c, g = i // groups, lax.rem(i, groups)
+        for j in range(LANES):
+            at = pl.ds(j, TILES, stride=LANES)
+            open_ref[GRID + j] = openings_ref[g, at, :]
+            even_ref[GRID + j] = cells_ref[g, pl.ds(c * size + j, TILES, stride=LANES), :]
+        fill_ends(open_ref, 0, LANES)
+        fill_ends(even_ref, 0, LANES)
+        store = storage_ref[i]
+        base = c * 4 * GRID
+        for j in range(LANES):
+            row, column = j // GRID, j % GRID
+            here = open_ref[GRID + j]
+            above, below = open_ref[j], open_ref[2 * GRID + j]
+            if row == 0:
+                above = jnp.where(top, here, above)
+            if row == LANES // GRID - 1:
+                below = jnp.where(bottom, here, below)
+            w_up, w_down = 0.5 * (here + above), 0.5 * (here + below)
+            w_left = here if column == 0 else 0.5 * (here + open_ref[GRID + j - 1])
+            w_right = here if column == GRID - 1 else 0.5 * (here + open_ref[GRID + j + 1])
+            inverse = 1.0 / (store + w_up + w_down + w_left + w_right)
+            value = sources_ref[g, pl.ds(c * size + j, TILES, stride=LANES), :] * inverse
+            w_up, w_down = w_up * inverse, w_down * inverse
+            w_left, w_right = w_left * inverse, w_right * inverse
+            if row == 0:
+                side = border_ref[g, pl.ds(base + column, 1), :]
+                value = value + jnp.where(top, w_up * side, 0.0)
+                w_up = jnp.where(top, 0.0, w_up)
+            if row == LANES // GRID - 1:
+                side = border_ref[g, pl.ds(base + GRID + column, 1), :]
+                value = value + jnp.where(bottom, w_down * side, 0.0)
+                w_down = jnp.where(bottom, 0.0, w_down)
+            step = LANES // GRID
+            if column == 0:
+                side = border_ref[g, pl.ds(base + 2 * GRID + row, TILES, stride=step), :]
+                value = value + w_left * side
+                w_left = jnp.zeros_like(w_left)
+            if column == GRID - 1:
+                side = border_ref[g, pl.ds(base + 3 * GRID + row, TILES, stride=step), :]
+                value = value + w_right * side
+                w_right = jnp.zeros_like(w_right)
+            s_ref[j] = value
+            up_ref[j], down_ref[j] = w_up, w_down
+            left_ref[j], right_ref[j] = w_left, w_right
+
+        def one_sweep(old, new):
+            for j in range(LANES):
+                new[GRID + j] = (s_ref[j] + up_ref[j] * old[j]) + (
+                    down_ref[j] * old[2 * GRID + j]
+                    + (left_ref[j] * old[GRID + j - 1] + right_ref[j] * old[GRID + j + 1])
+                )
+                fill_ends(new, j, 1)
+
+        def two_sweeps(k, carry):
+            one_sweep(even_ref, odd_ref)
+            one_sweep(odd_ref, even_ref)
+            return carry
+
+        lax.fori_loop(0, SWEEPS // 2, two_sweeps, 0)
+        for j in range(LANES):
+            new_ref[g, pl.ds(c * size + j, TILES, stride=LANES), :] = even_ref[GRID + j]
         return carry
 
-    lax.fori_loop(0, fracs // 8, one_tile, 0)
+    lax.fori_loop(0, 2 * groups, one_block, 0)
+    if not last:
+        take_edges(new_ref, new_edges_ref)
+        return
+    for c in range(2):
+        for g in range(groups):
+            for tile in range(TILES):
+                row = c * size + tile * LANES
+                cells = new_ref[g, row : row + LANES, :]
+                out_ref[tile_rows(g, tile, c), :] = jnp.transpose(cells)
 
 
 def call(body, shapes, scratch=(), **params):
@@ -375,7 +410,7 @@
         body,
         out_shape=[jax.ShapeDtypeStruct(shape, dtype) for shape, dtype in shapes],
         scratch_shapes=list(scratch),
-        compiler_params=pltpu.CompilerParams(vmem_limit_bytes=48 * 1024 * 1024, **params),
+        compiler_params=pltpu.CompilerParams(vmem_limit_bytes=40 * 1024 * 1024, **params),
     )
 
 
@@ -431,13 +466,22 @@
         functools.partial(slots_body, peers, fracs), [(table, i32)] * 3
     )(records)
     arrived = exchange(target)
-    state, sources = by_tiles(fields), by_tiles(source)
+    groups = fracs // LANES
+    turned = (groups, 2 * GRID * GRID, LANES)
+    edges_type = ((8 * GRID, fracs), f32)
+    cells, sources, openings, edges = call(
+        turn_body, [(turned, f32), (turned, f32), ((groups, GRID * GRID, LANES), f32), edges_type]
+    )(by_tiles(fields), by_tiles(source), aperture)
+    stores = storage.T.reshape(2 * groups, 1, LANES)
+    padded = pltpu.VMEM((LANES + 2 * GRID, TILES, LANES), f32)
+    block = pltpu.VMEM((LANES, TILES, LANES), f32)
     for step in range(ITERS):
-        edges, rows, mean = call(
-            functools.partial(edges_body, peers, fracs),
-            [((8 * GRID, fracs), f32), ((peers, 2 * GRID, SLOT), f32), (table, f32)],
+        last = step == ITERS - 1
+        rows, mean = call(
+            functools.partial(gather_body, peers, fracs),
+            [((peers, 2 * GRID, SLOT), f32), (table, f32)],
             [pltpu.VMEM((24 * GRID, fracs), jnp.bfloat16)],
-        )(state, sender)
+        )(edges, sender)
         rows, extra = call(
             functools.partial(traffic_body, peers, columns, fracs, high),
             [((peers, 2 * GRID, SLOT), f32), ((peers, 8, LANES), f32)],
@@ -451,16 +495,24 @@
             collective_id=0,
             has_side_effects=True,
         )(rows, mean, edges, arrived, index, weight)
-        (state,) = call(
-            functools.partial(sweep_body, peers, fracs, high),
-            [(state.shape, f32)],
+        results = call(
+            functools.partial(sweep_body, peers, fracs, high, last),
+            [((fracs * 2 * TILES, LANES), f32)] if last else [(turned, f32), edges_type],
             [
                 pltpu.VMEM((24 * GRID, fracs), f32),
                 pltpu.VMEM((16, fracs), f32),
-                pltpu.VMEM((2, fracs, 4 * GRID), f32),
-                pltpu.VMEM((2, fracs, GRID * GRID), f32),
-            ],
-        )(rows, extra, arrived, edges, state, aperture, sources, storage)
+                pltpu.VMEM((groups, 8 * GRID, LANES), f32),
+                padded,
+                padded,
+                padded,
+            ]
+            + [block] * 5
+            + ([pltpu.VMEM(turned, f32)] if last else []),
+        )(rows, extra, arrived, edges, cells, openings, sources, stores)
+        if last:
+            (state,) = results
+        else:
+            cells, edges = results
     coarse_out = extra.reshape(peers, 8 * LANES)[:, :per_dev].reshape(coarse)
     fields_out = state.reshape(fracs, TILES, 2, LANES).transpose(0, 2, 1, 3).reshape(fields.shape)
     return fields_out, coarse_out

time: 169 us -> 144 us (0.85)
  Pallas kernels: 154 us -> 107 us
  local copies, waits for them, and re-layouts: 4.95 us -> 26.1 us
    pallas_call x4 -> x5, Pallas kernels: 78.5 us -> 39.2 us  [the longest x2 31.4 us: shards(): call(functools.partial(sweep_body, peers, fracs, high, last), [((fracs *...]
    unnamed x6 -> x49, local copies, waits for them, and re-layouts: 2.43 us -> 20.2 us
    pallas_call x2, Pallas kernels: 73.4 us -> 65.2 us  [shards(): call(functools.partial(traffic_body, peers, columns, fracs, high), [((pee...]
  transfers between devices with their start and end apart: 1 -> 1, of which waited for: 0 -> 0; matrix products, arithmetic and copies ran while one was open for 1% -> 2% of each run, Pallas kernels for 3% -> 3%
where the time goes in v3:
time: 144 us; the launch traced here: 143 us
  Pallas kernels  107 us (74%)
  local copies, waits for them, and re-layouts  26.1 us (18%)
  starting transfers between devices  7.3 us (5%)
  other arithmetic  1.44 us (1%)
    pallas_call x2, Pallas kernels, shards(): call(functools.partial(traffic_body, peers, columns, fracs, high), [((pee...  65.2 us
    pallas_call x2, Pallas kernels, shards(): call(functools.partial(sweep_body, peers, fracs, high, last), [((fracs *...  31.4 us
    unnamed x49, local copies, waits for them, and re-layouts  20.2 us
    all_to_all x1, starting transfers between devices, exchange(): return lax.all_to_all(x, AXES, split_axis=0, concat_axis=0, tiled=True)  7.3 us
    pallas_call x2, Pallas kernels, shards(): call(functools.partial(gather_body, peers, fracs), [((peers, 2 * GRID, SL...  6.05 us
  transfers between devices with their start and end apart: 1, of which 0 were waited for; matrix products, arithmetic and copies ran while one was open for 2% of the time, Pallas kernels for 3%

profile of v3, /device:TPU:0, one launch (start us, length us, event | category | flops | bytes accessed | tf_op | source)
XLA Modules:
  0.0 142.7 jit_solution(702061932521126284)
XLA Ops:
  0.6 0.7 broadcast_add_fusion
  1.4 0.7 subtract_and_fusion
  2.1 1.0 stack.27.record_ref
  3.1 2.6 %shard_map.123 = (s32[32,128]{1,0:T(8,128)S(1)}, s32[32,128]{1,0:T(8,128)}, s32[32,128]{1,0:T(8,128)S(1)}) custom-call(s32[8,4096]{1,0:T(8,128)S(1)} %stack.27.record_ref), custom_call_target="tpu_custom_call" | custom-call | tf_op jit(solution)/shard_map/pallas_call | solution.py:465
  6.2 7.3 %all-to-all-start = ((s32[32,1,128]{2,1,0:T(1,128)}), s32[32,1,128]{2,1,0:T(1,128)S(1)}, u32[]{:S(2)}, u32[]{:S(2)}) async-start(s32[32,1,128]{2,1,0:T(1,128)} %bitcast.14), calls=%async_computation | async-start | bytes 32768 | tf_op jit(solution)/shard_map/all_to_all | solution.py:418
  13.5 0.8 dynamic_slice.3
  14.9 1.3 reshape.41.storage_ref
  16.2 1.6 %copy-done.4 = f32[256,2,1024]{2,1,0:T(2,128)S(1)} copy-done((f32[256,2,1024]{2,1,0:T(2,128)S(1)}, f32[256,2,1024]{2,1,0:T(2,128)}, u32[]{:S(2)}) %copy-start.4) | copy-done | bytes 2097176
  17.8 1.6 %copy-done.5 = f32[256,2,1024]{2,1,0:T(2,128)S(1)} copy-done((f32[256,2,1024]{2,1,0:T(2,128)S(1)}, f32[256,2,1024]{2,1,0:T(2,128)}, u32[]{:S(2)}) %copy-start.5) | copy-done | bytes 2097176
  19.4 1.2 copy-done.8
  20.6 1.8 %shard_map.122 = (f32[2,2048,128]{2,1,0:T(8,128)S(1)}, f32[2,2048,128]{2,1,0:T(8,128)S(1)}, f32[2,1024,128]{2,1,0:T(8,128)S(1)}, f32[256,256]{1,0:T(8,128)S(1)}) custom-call(f32[4096,128]{1,0:T(8,128)S(1)} %bitcast.33, f32[4096,128]{1,0:T(8,128)S(1)} %bitcast.34, f32[256,1024]{1,0:T(8,128)S(1)} %copy-done.8), custom_call_target="tpu_custom_call" | custom-call | tf_op jit(solution)/shard_map/pallas_call | solution.py:472
  22.4 1.3 copy-done.6
  23.7 3.0 %shard_map.124 = (f32[32,64,128]{2,1,0:T(8,128)S(1)}, f32[32,128]{1,0:T(8,128)S(1)}) custom-call(f32[256,256]{1,0:T(8,128)S(1)} %get-tuple-element.19.edges_ref, s32[32,128]{1,0:T(8,128)S(1)} %get-tuple-element.20.sender_ref), custom_call_target="tpu_custom_call" | custom-call | tf_op jit(solution)/shard_map/pallas_call | solution.py:480
  26.8 1.0 copy-done.11
  28.3 1.2 copy-done.12
  29.6 0.7 copy-done.14
  30.3 0.7 copy-done.18
  31.0 0.7 copy-done.23
  31.7 32.4 %shard_map.125 = (f32[32,64,128]{2,1,0:T(8,128)S(1)}, f32[32,8,128]{2,1,0:T(8,128)S(1)}) custom-call(f32[32,64,128]{2,1,0:T(8,128)S(1)} %copy-done.12, f32[32,128]{1,0:T(8,128)S(1)} %copy-done.23, f32[256,256]{1,0:T(8,128)S(1)} %get-tuple-element.19.edges_ref, s32[32,128]{1,0:T(8,128)S(1)} %bitcast.36, s32[32,128]{1,0:T(8,128)S(1)} %copy-done.14, ...), custom_call_target="tpu_custom_call" | custom-call | tf_op jit(solution)/shard_map/pallas_call | solution.py:485
  64.1 0.9 copy-done.1
  65.0 1.6 %copy-done.7 = f32[2,2048,128]{2,1,0:T(8,128)S(1)} copy-done((f32[2,2048,128]{2,1,0:T(8,128)S(1)}, f32[2,2048,128]{2,1,0:T(8,128)}, u32[]{:S(2)}) %copy-start.7) | copy-done | bytes 2097176
  66.6 0.7 copy-done.20
  67.3 14.7 %shard_map.126 = (f32[2,2048,128]{2,1,0:T(8,128)S(1)}, f32[256,256]{1,0:T(8,128)S(1)}) custom-call(f32[32,64,128]{2,1,0:T(8,128)S(1)} %get-tuple-element.25.rows_ref, f32[32,8,128]{2,1,0:T(8,128)S(1)} %get-tuple-element.26.extra_ref, s32[32,128]{1,0:T(8,128)S(1)} %bitcast.37, f32[256,256]{1,0:T(8,128)S(1)} %copy-done.1, f32[2,2048,128]{2,1,0:T(8,128)S(1)} %copy-done.7, ...), custom_call_target="tpu_custom_call" | custom-call | tf_op jit(solution)/shard_map/pallas_call | solution.py:498
  82.0 1.3 copy-done.2
  83.3 3.0 %shard_map.127 = (f32[32,64,128]{2,1,0:T(8,128)S(1)}, f32[32,128]{1,0:T(8,128)S(1)}) custom-call(f32[256,256]{1,0:T(8,128)S(1)} %get-tuple-element.30.edges_ref, s32[32,128]{1,0:T(8,128)S(1)} %copy-done.17), custom_call_target="tpu_custom_call" | custom-call | tf_op jit(solution)/shard_map/pallas_call | solution.py:480
  86.4 32.8 %shard_map.128 = (f32[32,64,128]{2,1,0:T(8,128)S(1)}, f32[32,8,128]{2,1,0:T(8,128)S(1)}) custom-call(f32[32,64,128]{2,1,0:T(8,128)S(1)} %get-tuple-element.31.rows_ref, f32[32,128]{1,0:T(8,128)S(1)} %get-tuple-element.32.mean_ref, f32[256,256]{1,0:T(8,128)S(1)} %get-tuple-element.30.edges_ref, s32[32,128]{1,0:T(8,128)S(1)} %bitcast.38, ...), custom_call_target="tpu_custom_call" | custom-call | tf_op jit(solution)/shard_map/pallas_call | solution.py:485
  119.2 1.0 copy-done.9
  120.8 1.7 %reshape.45 = f32[25088]{0:T(1024)} reshape(f32[32,784]{1,0:T(8,128)} %slice.4) | data formatting | bytes 200704 | tf_op jit(solution)/shard_map/reshape | solution.py:516
  122.5 1.6 %copy-done.3 = f32[2,2048,128]{2,1,0:T(8,128)S(1)} copy-done((f32[2,2048,128]{2,1,0:T(8,128)S(1)}, f32[2,2048,128]{2,1,0:T(8,128)}, u32[]{:S(2)}) %copy-start.3) | copy-done | bytes 2097176
  124.1 1.2 copy-done.10
  125.3 0.7 copy-done.21
  126.0 16.7 %shard_map.129 = f32[4096,128]{1,0:T(8,128)} custom-call(f32[32,64,128]{2,1,0:T(8,128)S(1)} %copy-done.10, f32[32,8,128]{2,1,0:T(8,128)S(1)} %get-tuple-element.34.extra_ref, s32[32,128]{1,0:T(8,128)S(1)} %bitcast.39, f32[256,256]{1,0:T(8,128)S(1)} %get-tuple-element.30.edges_ref, f32[2,2048,128]{2,1,0:T(8,128)S(1)} %copy-done.3, ...), custom_call_target="tpu_custom_call" | custom-call | tf_op jit(solution)/shard_map/pallas_call | solution.py:498
  (36 shorter events, 2.5 us)
Async XLA Ops:
  5.6 0.6 copy-start.13
  6.2 17.5 %copy-start.16 = (s32[32,128]{1,0:T(8,128)}, s32[32,128]{1,0:T(8,128)S(1)}, u32[]{:S(2)}) copy-start(s32[32,128]{1,0:T(8,128)S(1)} %get-tuple-element.20.sender_ref) | copy-start | bytes 49156
  6.2 22.1 %all-to-all-start = ((s32[32,1,128]{2,1,0:T(1,128)}), s32[32,1,128]{2,1,0:T(1,128)S(1)}, u32[]{:S(2)}, u32[]{:S(2)}) async-start(s32[32,1,128]{2,1,0:T(1,128)} %bitcast.14), calls=%async_computation | async-start | bytes 32768 | tf_op jit(solution)/shard_map/all_to_all | solution.py:418
  16.2 1.6 %copy-start.4 = (f32[256,2,1024]{2,1,0:T(2,128)S(1)}, f32[256,2,1024]{2,1,0:T(2,128)}, u32[]{:S(2)}) copy-start(f32[256,2,1024]{2,1,0:T(2,128)} %param.11) | copy-start | bytes 6291460
  17.8 1.6 %copy-start.5 = (f32[256,2,1024]{2,1,0:T(2,128)S(1)}, f32[256,2,1024]{2,1,0:T(2,128)}, u32[]{:S(2)}) copy-start(f32[256,2,1024]{2,1,0:T(2,128)} %param.13) | copy-start | bytes 6291460
  19.4 1.2 copy-start.8
  22.4 1.3 copy-start.6
  23.7 40.3 %copy-start = (f32[256,256]{1,0:T(8,128)}, f32[256,256]{1,0:T(8,128)S(1)}, u32[]{:S(2)}) copy-start(f32[256,256]{1,0:T(8,128)S(1)} %get-tuple-element.19.edges_ref) | copy-start | bytes 786436
  26.8 1.0 copy-start.11
  27.7 0.6 copy-start.22
  28.3 1.2 copy-start.12
  29.6 0.7 copy-start.14
  30.3 0.7 copy-start.18
  31.0 0.7 copy-start.23
  64.1 1.0 copy-start.1
  65.0 1.6 %copy-start.7 = (f32[2,2048,128]{2,1,0:T(8,128)S(1)}, f32[2,2048,128]{2,1,0:T(8,128)}, u32[]{:S(2)}) copy-start(f32[2,2048,128]{2,1,0:T(8,128)} %copy-done.6) | copy-start | bytes 6291460
  66.6 0.7 copy-start.20
  67.3 16.1 %copy-start.17 = (s32[32,128]{1,0:T(8,128)S(1)}, s32[32,128]{1,0:T(8,128)}, u32[]{:S(2)}) copy-start(s32[32,128]{1,0:T(8,128)} %copy-done.16) | copy-start | bytes 49156
  67.3 19.1 %copy-start.15 = (s32[32,128]{1,0:T(8,128)S(1)}, s32[32,128]{1,0:T(8,128)}, u32[]{:S(2)}) copy-start(s32[32,128]{1,0:T(8,128)} %copy-done.13) | copy-start | bytes 49156
  67.3 19.1 %copy-start.19 = (f32[8,128]{1,0:T(8,128)S(1)}, f32[8,128]{1,0:T(8,128)}, u32[]{:S(2)}) copy-start(f32[8,128]{1,0:T(8,128)} %pad_bitcast_fusion.weight_ref) | copy-start | bytes 12292
  82.0 1.3 copy-start.2
  119.2 1.0 copy-start.9
  122.5 1.6 %copy-start.3 = (f32[2,2048,128]{2,1,0:T(8,128)S(1)}, f32[2,2048,128]{2,1,0:T(8,128)}, u32[]{:S(2)}) copy-start(f32[2,2048,128]{2,1,0:T(8,128)} %copy-done.2) | copy-start | bytes 6291460
  124.1 1.2 copy-start.10
  125.3 0.7 copy-start.21
